TPU v7x, 32 devices: a whole 2x2x4 slice. The times are simulated.
32 devices in a mesh: brick: 8 (over z, y), region: 4 (over x, core).
Axes of the slice: x: 2, y: 2, z: 4, core: 2. Of those that a mesh axis runs over, the one named last changes fastest.
Arguments:
- micrograph: bfloat16 [4, 8, 512], P('region', 'brick'), may hold values from -6 to 6
- tissue: int32 [4, 8], P('region', 'brick'), may hold values from 0 to 1, as said below
- neighbours: int32 [4, 8, 26], P('region', 'brick'), may hold values from -1 to 7, as said below
- first_weight: bfloat16 [64, 27], replicated, may hold values from -1.25 to 1.25
- first_bias: float32 [64], replicated, may hold values from -3 to 3
- second_weight: bfloat16 [64, 1728], replicated, may hold values from -0.15625 to 0.15625
- second_bias: float32 [64], replicated, may hold values from -3 to 3
- head_weight: bfloat16 [4, 64], replicated, may hold values from -0.75 to 0.75
- head_bias: float32 [4], replicated, may hold values from -3 to 3
- cotangent: bfloat16 [4, 8, 4, 512], P('region', 'brick'), may hold values from -6 to 6
Outputs:
- prediction: bfloat16 [4, 8, 4, 512], P('region', 'brick')
- first_weight_grad: float32 [64, 27], replicated
- first_bias_grad: float32 [64], replicated
- second_weight_grad: float32 [64, 1728], replicated
- second_bias_grad: float32 [64], replicated
- head_weight_grad: float32 [4, 64], replicated
- head_bias_grad: float32 [4], replicated
Inputs may be any that keep to these rules, and one draw needn't show every extreme that they name: 1 marks a slot that holds a tissue brick, 0 an empty slot whose outputs are zero. `neighbours`: an entry is -1 or the index, in the same region, of a tissue brick that touches the brick in that direction; empty slots list -1 only; the lists are symmetric (if brick n lists m in direction (a, b, c), m lists n in direction (-a, -b, -c)); every entry in a direction with b ≠ 0 is -1 (a region is one brick thick along y); a brick m listed by n in direction (a, 0, c) has m = n + 2 a + c, so its device is at most 3 away, and in every draw some brick lists one whose device is exactly 3 away.
All inputs are finite; a program needn't handle non-finite values.
Results may differ from a plain program's by a relative error of at most 0.015.
Values may be sent and summed in bfloat16 or wider, within the bound.
A program may use at most 64 MiB of HBM per device.

v0:
```python
from functools import partial

import jax
import jax.numpy as jnp
from jax import lax
from jax.sharding import PartitionSpec as P

EDGE = 8
TAPS = 27
REACH = 3


DIRECTIONS = [
    (shift_x, shift_y, shift_z)
    for shift_x in (-1, 0, 1)
    for shift_y in (-1, 0, 1)
    for shift_z in (-1, 0, 1)
    if (shift_x, shift_y, shift_z) != (0, 0, 0)
]
TAP_OFFSETS = [
    (shift_x, shift_y, shift_z)
    for shift_x in (-1, 0, 1)
    for shift_y in (-1, 0, 1)
    for shift_z in (-1, 0, 1)
]


def passed_along(block, axis, distance):
    devices = range(lax.axis_size(axis))
    route = [(i - distance, i) for i in devices if i - distance in devices]
    return lax.ppermute(block, axis, route)


def face_table(volume, margin):
    side_len = volume.shape[-1]
    sections = [
        volume[:, :, :margin],
        volume[:, :, side_len - margin :],
        volume[:, :, :, :margin],
        volume[:, :, :, side_len - margin :],
        volume[:, :, :, :, :margin],
        volume[:, :, :, :, side_len - margin :],
    ]
    return jnp.concatenate(
        [section.reshape(section.shape[0], section.shape[1], -1) for section in sections], axis=2
    )


def assemble(volume, table, row_index, present, margin):
    number, channels, side_len = (volume.shape[0], volume.shape[1], volume.shape[2])
    face_size = margin * side_len * side_len
    pieces = {(0, 0, 0): volume}
    for dir_index, direction in enumerate(DIRECTIONS):
        normal = [axis_id for axis_id in range(3) if direction[axis_id] != 0][0]
        face_index = 2 * normal + (0 if direction[normal] > 0 else 1)
        selected = jnp.take(
            table[:, :, face_index * face_size : (face_index + 1) * face_size],
            row_index[:, dir_index],
            axis=0,
        )
        extent = [side_len, side_len, side_len]
        extent[normal] = margin
        selected = selected.reshape((number, channels) + tuple(extent))
        sources = []
        for axis_id in range(3):
            if axis_id == normal or direction[axis_id] > 0:
                sources.append(slice(0, margin))
            elif direction[axis_id] < 0:
                sources.append(slice(side_len - margin, side_len))
            else:
                sources.append(slice(0, side_len))
        portion = selected[:, :, sources[0], sources[1], sources[2]]
        presence = present[:, dir_index].astype(portion.dtype).reshape(number, 1, 1, 1, 1)
        pieces[direction] = portion * presence
    planes = []
    for shift_x in (-1, 0, 1):
        lines = []
        for shift_y in (-1, 0, 1):
            lines.append(
                jnp.concatenate(
                    [pieces[shift_x, shift_y, shift_z] for shift_z in (-1, 0, 1)], axis=4
                )
            )
        planes.append(jnp.concatenate(lines, axis=3))
    return jnp.concatenate(planes, axis=2)


def window_group(padded, margin, out_len, sign, group_id):
    number, inputs = (padded.shape[0], padded.shape[1])
    views = []
    for offset in TAP_OFFSETS[9 * group_id : 9 * group_id + 9]:
        start_x, start_y, start_z = [margin + sign * value for value in offset]
        views.append(
            padded[
                :,
                :,
                start_x : start_x + out_len,
                start_y : start_y + out_len,
                start_z : start_z + out_len,
            ].reshape(number, inputs, -1)
        )
    return jnp.concatenate(views, axis=1)


def convolve(padded, blocks, margin, out_len, sign):
    inputs = padded.shape[1]
    outputs_ch = blocks.shape[1]
    running = None
    for group_id in range(3):
        stacked = window_group(padded, margin, out_len, sign, group_id)
        grouped = (
            blocks[9 * group_id : 9 * group_id + 9]
            .transpose(1, 0, 2)
            .reshape(outputs_ch, 9 * inputs)
        )
        contrib = jnp.einsum("oj,njp->nop", grouped, stacked, preferred_element_type=jnp.float32)
        running = contrib if running is None else running + contrib
    return running


def tap_grads(left, padded, margin, out_len, exact):
    columns = []
    for group_id in range(3):
        stacked = window_group(padded, margin, out_len, 1, group_id)
        if exact:
            columns.append(
                jnp.einsum(
                    "nop,njp->oj",
                    left,
                    stacked.astype(jnp.float32),
                    precision=lax.Precision.HIGHEST,
                )
            )
        else:
            columns.append(
                jnp.einsum("nop,njp->oj", left, stacked, preferred_element_type=jnp.float32)
            )
    return jnp.concatenate(columns, axis=1)


def gelu_slope(values):
    _, backward = jax.vjp(partial(jax.nn.gelu, approximate=True), values)
    return backward(jnp.ones_like(values))[0]


def em_window(faces):
    parts_list = []
    for offset in range(-REACH, REACH + 1):
        if offset == 0:
            parts_list.append(faces)
        else:
            parts_list.append(passed_along(faces, "brick", -offset))
    return jnp.concatenate(parts_list, axis=0)


def first_window(faces):
    parts_list = []
    for offset in range(-REACH, REACH + 1):
        if offset == 0:
            parts_list.append(faces)
        else:
            parts_list.append(passed_along(faces, "brick", -offset))
    return jnp.concatenate(parts_list, axis=0)


def grad_window(faces):
    parts_list = []
    for offset in range(-REACH, REACH + 1):
        if offset == 0:
            parts_list.append(faces)
        else:
            parts_list.append(passed_along(faces, "brick", -offset))
    return jnp.concatenate(parts_list, axis=0)


def shards(
    micrograph,
    tissue,
    neighbours,
    first_weight,
    first_bias,
    second_weight,
    second_bias,
    head_weight,
    head_bias,
    cotangent,
):
    number = micrograph.shape[1]
    channels = first_weight.shape[0]
    position = lax.axis_index("brick")
    neighbour_ids = neighbours[0]
    present = neighbour_ids >= 0
    holder = jnp.where(present, neighbour_ids // number, position)
    row_index = jnp.where(present, (holder - position + REACH) * number + neighbour_ids % number, 0)
    active = tissue[0].astype(jnp.float32).reshape(number, 1, 1)
    blocks_first = first_weight.T[:, :, None]
    blocks_second = second_weight.reshape(channels, TAPS, channels).transpose(1, 0, 2)
    blocks_back = blocks_second.transpose(0, 2, 1)
    volume = micrograph[0].reshape(number, 1, EDGE, EDGE, EDGE)
    em_pad = assemble(volume, em_window(face_table(volume, 1)), row_index, present, 1)
    z_first = convolve(em_pad, blocks_first, 1, EDGE, 1) + first_bias[None, :, None]
    h_first = (jax.nn.gelu(z_first, approximate=True) * active).astype(jnp.bfloat16)
    cube_first = h_first.reshape(number, channels, EDGE, EDGE, EDGE)
    first_table = first_window(face_table(cube_first, 1))
    first_pad = assemble(cube_first, first_table, row_index, present, 1)
    z_second = convolve(first_pad, blocks_second, 1, EDGE, 1) + second_bias[None, :, None]
    h_second = (jax.nn.gelu(z_second, approximate=True) * active).astype(jnp.bfloat16)
    linear = (
        jnp.einsum("kc,ncp->nkp", head_weight, h_second, preferred_element_type=jnp.float32)
        + head_bias[None, :, None]
    )
    prediction = (linear * active).astype(jnp.bfloat16)
    total_bricks = lax.axis_size("brick") * number * lax.axis_size("region")
    dpred = (cotangent[0].astype(jnp.float32) * active / total_bricks).astype(jnp.bfloat16)
    grad_wh = jnp.einsum("nkp,ncp->kc", dpred, h_second, preferred_element_type=jnp.float32)
    grad_bh = jnp.sum(dpred.astype(jnp.float32), axis=(0, 2))
    dh_second = jnp.einsum("kc,nkp->ncp", head_weight, dpred, preferred_element_type=jnp.float32)
    dz_second = (dh_second * gelu_slope(z_second) * active).astype(jnp.bfloat16)
    grad_w2 = tap_grads(dz_second, first_pad, 1, EDGE, False)
    grad_b2 = jnp.sum(dz_second.astype(jnp.float32), axis=(0, 2))
    cube_grad = dz_second.reshape(number, channels, EDGE, EDGE, EDGE)
    grad_table = grad_window(face_table(cube_grad, 1))
    grad_pad = assemble(cube_grad, grad_table, row_index, present, 1)
    dh_first = convolve(grad_pad, blocks_back, 1, EDGE, -1)
    dz_first = dh_first * gelu_slope(z_first) * active
    grad_w1 = tap_grads(dz_first, em_pad, 1, EDGE, True)
    grad_b1 = jnp.sum(dz_first, axis=(0, 2))
    grad_w1, grad_b1, grad_w2, grad_b2, grad_wh, grad_bh = lax.psum(
        (grad_w1, grad_b1, grad_w2, grad_b2, grad_wh, grad_bh), ("brick", "region")
    )
    return (prediction[None], grad_w1, grad_b1, grad_w2, grad_b2, grad_wh, grad_bh)


def solution(mesh):
    return jax.shard_map(
        shards,
        mesh=mesh,
        in_specs=(
            P("region", "brick", None),
            P("region", "brick"),
            P("region", "brick", None),
            P(),
            P(),
            P(),
            P(),
            P(),
            P(),
            P("region", "brick", None, None),
        ),
        out_specs=(P("region", "brick", None, None), P(), P(), P(), P(), P(), P()),
        check_vma=False,
    )
```

profile of v0, /device:TPU:0, one launch (start us, length us, event | category | flops | bytes accessed | tf_op | source)
XLA Modules:
  0.0 312.2 jit_solution(9217967433930259066)
XLA Ops:
  7.2 0.7 reduce.1
  8.9 1.3 collective-permute-start.5
  10.2 1.3 collective-permute-start.4
  11.5 1.3 collective-permute-start.3
  12.8 5.5 %collective-permute-start.2 = (bf16[1,1,384]{2,1,0:T(2,128)(2,1)S(1)}, bf16[1,1,384]{2,1,0:T(2,128)(2,1)S(1)}, u32[]{:S(2)}, u32[]{:S(2)}) collective-permute-start(bf16[1,1,384]{2,1,0:T(2,128)(2,1)S(1)} %concatenate.282), channel_id=1, source_target_pairs={{0,4},{4,8},{8,12},{12,16},{16,20},{20,24},{24,28},{1,5},{5,9},{9,... | collective-permute-start | bytes 2312 | tf_op jit(solution)/shard_map/ppermute | solution.py:31
  18.3 7.1 %collective-permute-start = (bf16[1,1,384]{2,1,0:T(2,128)(2,1)S(1)}, bf16[1,1,384]{2,1,0:T(2,128)(2,1)S(1)}, u32[]{:S(2)}, u32[]{:S(2)}) collective-permute-start(bf16[1,1,384]{2,1,0:T(2,128)(2,1)S(1)} %concatenate.282), channel_id=1, source_target_pairs={{0,12},{4,16},{8,20},{12,24},{16,28},{1,13},{5,17},{9,21},{13,25},... | collective-permute-start | bytes 2312 | tf_op jit(solution)/shard_map/ppermute | solution.py:31
  25.4 0.6 copy-done.30
  26.1 0.6 fusion.235
  40.3 0.7 fusion.233
  77.7 0.7 fusion.234
  78.3 0.7 fusion.232
  97.3 3.9 %collective-permute-start.1 = (bf16[1,1,384]{2,1,0:T(2,128)(2,1)S(1)}, bf16[1,1,384]{2,1,0:T(2,128)(2,1)S(1)}, u32[]{:S(2)}, u32[]{:S(2)}) collective-permute-start(bf16[1,1,384]{2,1,0:T(2,128)(2,1)S(1)} %concatenate.282), channel_id=1, source_target_pairs={{0,8},{4,12},{8,16},{12,20},{16,24},{20,28},{1,9},{5,13},{9,17},{1... | collective-permute-start | bytes 2312 | tf_op jit(solution)/shard_map/ppermute | solution.py:31
  101.3 1.3 collective-permute-done.1
  102.9 0.7 slice.1088
  103.7 0.6 slice.1111
  104.5 0.6 slice.1105
  105.4 0.6 slice.1094
  106.5 0.6 slice.1016
  107.4 0.5 slice.1039
  108.1 0.6 slice.1033
  109.0 0.5 slice.1022
  119.2 0.6 copy-done.27
  121.2 0.7 copy-done.31
  121.8 0.9 multiply_convert_fusion.1
  123.0 5.5 %collective-permute-start.6 = (bf16[1,64,384]{1,2,0:T(8,128)(2,1)S(1)}, bf16[1,64,384]{1,2,0:T(8,128)(2,1)S(1)}, u32[]{:S(2)}, u32[]{:S(2)}) collective-permute-start(bf16[1,64,384]{1,2,0:T(8,128)(2,1)S(1)} %constant_dynamic-update-slice_fusion.7), channel_id=1, source_target_pairs={{0,12},{4,16},{8,20},{12,24},{16,28},{1,13},{5,17},{9,21},{13,25},... | collective-permute-start | bytes 147464 | tf_op jit(solution)/shard_map/ppermute | solution.py:31
  129.6 1.3 collective-permute-start.11
  130.8 1.3 collective-permute-start.10
  132.2 1.3 collective-permute-start.9
  133.4 4.6 %collective-permute-start.8 = (bf16[1,64,384]{1,2,0:T(8,128)(2,1)S(1)}, bf16[1,64,384]{1,2,0:T(8,128)(2,1)S(1)}, u32[]{:S(2)}, u32[]{:S(2)}) collective-permute-start(bf16[1,64,384]{1,2,0:T(8,128)(2,1)S(1)} %constant_dynamic-update-slice_fusion.7), channel_id=1, source_target_pairs={{0,4},{4,8},{8,12},{12,16},{16,20},{20,24},{24,28},{1,5},{5,9},{9,... | collective-permute-start | bytes 147464 | tf_op jit(solution)/shard_map/ppermute | solution.py:31
  138.0 4.6 %collective-permute-start.7 = (bf16[1,64,384]{1,2,0:T(8,128)(2,1)S(1)}, bf16[1,64,384]{1,2,0:T(8,128)(2,1)S(1)}, u32[]{:S(2)}, u32[]{:S(2)}) collective-permute-start(bf16[1,64,384]{1,2,0:T(8,128)(2,1)S(1)} %constant_dynamic-update-slice_fusion.7), channel_id=1, source_target_pairs={{0,8},{4,12},{8,16},{12,20},{16,24},{20,28},{1,9},{5,13},{9,17},{1... | collective-permute-start | bytes 147464 | tf_op jit(solution)/shard_map/ppermute | solution.py:31
  142.7 2.2 collective-permute-done.7
  145.8 0.7 copy.57
  147.1 0.7 copy.60
  147.8 0.7 copy.59
  148.5 0.7 copy.58
  150.6 1.0 fusion.218
  151.6 0.8 copy-done.15
  152.4 0.8 copy-done.14
  153.2 0.8 copy-done.13
  154.9 0.9 convolution_add_fusion.3
  156.1 1.3 concatenate.327
  157.4 0.6 copy-done.29
  159.8 1.3 collective-permute-start.17
  161.1 1.3 collective-permute-start.16
  162.4 1.3 collective-permute-start.15
  163.7 5.6 %collective-permute-start.14 = (bf16[1,64,384]{1,2,0:T(8,128)(2,1)S(1)}, bf16[1,64,384]{1,2,0:T(8,128)(2,1)S(1)}, u32[]{:S(2)}, u32[]{:S(2)}) collective-permute-start(bf16[1,64,384]{1,2,0:T(8,128)(2,1)S(1)} %constant_dynamic-update-slice_fusion.34), channel_id=1, source_target_pairs={{0,4},{4,8},{8,12},{12,16},{16,20},{20,24},{24,28},{1,5},{5,9},{9,... | collective-permute-start | bytes 147464 | tf_op jit(solution)/shard_map/ppermute | solution.py:31
  169.4 7.9 %collective-permute-start.12 = (bf16[1,64,384]{1,2,0:T(8,128)(2,1)S(1)}, bf16[1,64,384]{1,2,0:T(8,128)(2,1)S(1)}, u32[]{:S(2)}, u32[]{:S(2)}) collective-permute-start(bf16[1,64,384]{1,2,0:T(8,128)(2,1)S(1)} %constant_dynamic-update-slice_fusion.34), channel_id=1, source_target_pairs={{0,12},{4,16},{8,20},{12,24},{16,28},{1,13},{5,17},{9,21},{13,25},... | collective-permute-start | bytes 147464 | tf_op jit(solution)/shard_map/ppermute | solution.py:31
  177.3 0.9 concatenate.352
  178.3 0.5 copy-done.32
  178.9 0.7 fusion.15
  180.0 4.3 %collective-permute-start.13 = (bf16[1,64,384]{1,2,0:T(8,128)(2,1)S(1)}, bf16[1,64,384]{1,2,0:T(8,128)(2,1)S(1)}, u32[]{:S(2)}, u32[]{:S(2)}) collective-permute-start(bf16[1,64,384]{1,2,0:T(8,128)(2,1)S(1)} %constant_dynamic-update-slice_fusion.34), channel_id=1, source_target_pairs={{0,8},{4,12},{8,16},{12,20},{16,24},{20,28},{1,9},{5,13},{9,17},{1... | collective-permute-start | bytes 147464 | tf_op jit(solution)/shard_map/ppermute | solution.py:31
  184.3 2.2 collective-permute-done.13
  188.4 0.7 copy.81
  189.1 0.7 copy.80
  191.0 0.9 fusion.216
  191.9 0.8 copy-done.17
  192.7 0.8 copy-done.16
  193.6 0.5 concatenate.339
  194.8 0.6 copy-done.1
  197.4 0.6 copy-done.22
  198.1 0.6 copy-done.20
  198.9 42.8 %all-reduce = (f32[64,27]{0,1:T(8,128)}, f32[64]{0:T(128)}, f32[64]{0:T(128)}, f32[4,64]{1,0:T(4,128)}, f32[4]{0:T(128)}) all-reduce(f32[64,27]{0,1:T(8,128)S(1)} %pad_maximum_fusion.7, f32[64]{0:T(128)S(1)} %get-tuple-element.276, f32[64]{0:T(128)S(1)} %get-tuple-element.278, ...), channel_id=1, replica_groups=mesh['brick'=8,'region'=4] {'brick','region'}, use_global_device_ids=true, to_apply=%region_0.3 | all-reduce | flops 2116 | bytes 16928 | tf_op jit(solution)/shard_map/psum | solution.py:228
  241.7 61.9 %all-reduce.3.cloned.1.call-done = f32[64,1728]{1,0:T(8,128)} async-done(((f32[64,1728]{1,0:T(8,128)}), f32[64,1728]{1,0:T(8,128)}) %all-reduce.3.cloned.1.call-update) | async-done | bytes 442384 | tf_op jit(solution)/shard_map/psum | solution.py:228
  303.5 1.8 copy.157
  (345 shorter events, 22.3 us)
Async XLA Ops:
  7.2 151.3 %copy-start = (bf16[4,64]{1,0:T(4,128)(2,1)S(1)}, bf16[4,64]{1,0:T(4,128)(2,1)}, u32[]{:S(2)}) copy-start(bf16[4,64]{1,0:T(4,128)(2,1)} %param.21) | copy-start | bytes 1540
  7.2 296.4 %all-reduce.3.cloned.1.call-start = ((), (), s32[]{:S(2)}) async-start(), calls=%async_computation | async-start | bytes 917504 | tf_op jit(solution)/shard_map/psum | solution.py:228
  8.9 93.7 %collective-permute-start.5 = (bf16[1,1,384]{2,1,0:T(2,128)(2,1)S(1)}, bf16[1,1,384]{2,1,0:T(2,128)(2,1)S(1)}, u32[]{:S(2)}, u32[]{:S(2)}) collective-permute-start(bf16[1,1,384]{2,1,0:T(2,128)(2,1)S(1)} %concatenate.282), channel_id=1, source_target_pairs={{12,0},{16,4},{20,8},{24,12},{28,16},{13,1},{17,5},{21,9},{25,13},... | collective-permute-start | bytes 2312 | tf_op jit(solution)/shard_map/ppermute | solution.py:31
  10.2 92.4 %collective-permute-start.4 = (bf16[1,1,384]{2,1,0:T(2,128)(2,1)S(1)}, bf16[1,1,384]{2,1,0:T(2,128)(2,1)S(1)}, u32[]{:S(2)}, u32[]{:S(2)}) collective-permute-start(bf16[1,1,384]{2,1,0:T(2,128)(2,1)S(1)} %concatenate.282), channel_id=1, source_target_pairs={{8,0},{12,4},{16,8},{20,12},{24,16},{28,20},{9,1},{13,5},{17,9},{2... | collective-permute-start | bytes 2312 | tf_op jit(solution)/shard_map/ppermute | solution.py:31
  11.5 91.1 %collective-permute-start.3 = (bf16[1,1,384]{2,1,0:T(2,128)(2,1)S(1)}, bf16[1,1,384]{2,1,0:T(2,128)(2,1)S(1)}, u32[]{:S(2)}, u32[]{:S(2)}) collective-permute-start(bf16[1,1,384]{2,1,0:T(2,128)(2,1)S(1)} %concatenate.282), channel_id=1, source_target_pairs={{4,0},{8,4},{12,8},{16,12},{20,16},{24,20},{28,24},{5,1},{9,5},{13... | collective-permute-start | bytes 2312 | tf_op jit(solution)/shard_map/ppermute | solution.py:31
  12.8 89.8 %collective-permute-start.2 = (bf16[1,1,384]{2,1,0:T(2,128)(2,1)S(1)}, bf16[1,1,384]{2,1,0:T(2,128)(2,1)S(1)}, u32[]{:S(2)}, u32[]{:S(2)}) collective-permute-start(bf16[1,1,384]{2,1,0:T(2,128)(2,1)S(1)} %concatenate.282), channel_id=1, source_target_pairs={{0,4},{4,8},{8,12},{12,16},{16,20},{20,24},{24,28},{1,5},{5,9},{9,... | collective-permute-start | bytes 2312 | tf_op jit(solution)/shard_map/ppermute | solution.py:31
  18.3 79.0 %collective-permute-start = (bf16[1,1,384]{2,1,0:T(2,128)(2,1)S(1)}, bf16[1,1,384]{2,1,0:T(2,128)(2,1)S(1)}, u32[]{:S(2)}, u32[]{:S(2)}) collective-permute-start(bf16[1,1,384]{2,1,0:T(2,128)(2,1)S(1)} %concatenate.282), channel_id=1, source_target_pairs={{0,12},{4,16},{8,20},{12,24},{16,28},{1,13},{5,17},{9,21},{13,25},... | collective-permute-start | bytes 2312 | tf_op jit(solution)/shard_map/ppermute | solution.py:31
  25.4 0.7 copy-start.30
  33.8 62.4 %copy-start.18 = (bf16[64,1728]{1,0:T(8,128)(2,1)S(1)}, bf16[64,1728]{1,0:T(8,128)(2,1)}, u32[]{:S(2)}) copy-start(bf16[64,1728]{1,0:T(8,128)(2,1)} %param.19) | copy-start | bytes 663556
  97.3 5.2 %collective-permute-start.1 = (bf16[1,1,384]{2,1,0:T(2,128)(2,1)S(1)}, bf16[1,1,384]{2,1,0:T(2,128)(2,1)S(1)}, u32[]{:S(2)}, u32[]{:S(2)}) collective-permute-start(bf16[1,1,384]{2,1,0:T(2,128)(2,1)S(1)} %concatenate.282), channel_id=1, source_target_pairs={{0,8},{4,12},{8,16},{12,20},{16,24},{20,28},{1,9},{5,13},{9,17},{1... | collective-permute-start | bytes 2312 | tf_op jit(solution)/shard_map/ppermute | solution.py:31
  119.1 0.7 copy-start.27
  119.1 0.8 copy-start.19
  119.8 0.7 copy-start.28
  120.5 0.6 copy-start.21
  121.2 1.6 copy-start.24
  121.2 0.7 copy-start.31
  123.0 5.6 %copy-start.26 = (bf16[1,1,4,512]{3,2,1,0:T(4,128)(2,1)S(1)}, bf16[1,1,4,512]{3,2,1,0:T(4,128)(2,1)}, u32[]{:S(2)}) copy-start(bf16[1,1,4,512]{3,2,1,0:T(4,128)(2,1)} %param.23) | copy-start | bytes 12292
  123.0 15.0 %collective-permute-start.6 = (bf16[1,64,384]{1,2,0:T(8,128)(2,1)S(1)}, bf16[1,64,384]{1,2,0:T(8,128)(2,1)S(1)}, u32[]{:S(2)}, u32[]{:S(2)}) collective-permute-start(bf16[1,64,384]{1,2,0:T(8,128)(2,1)S(1)} %constant_dynamic-update-slice_fusion.7), channel_id=1, source_target_pairs={{0,12},{4,16},{8,20},{12,24},{16,28},{1,13},{5,17},{9,21},{13,25},... | collective-permute-start | bytes 147464 | tf_op jit(solution)/shard_map/ppermute | solution.py:31
  129.6 15.5 %collective-permute-start.11 = (bf16[1,64,384]{1,2,0:T(8,128)(2,1)S(1)}, bf16[1,64,384]{1,2,0:T(8,128)(2,1)S(1)}, u32[]{:S(2)}, u32[]{:S(2)}) collective-permute-start(bf16[1,64,384]{1,2,0:T(8,128)(2,1)S(1)} %constant_dynamic-update-slice_fusion.7), channel_id=1, source_target_pairs={{12,0},{16,4},{20,8},{24,12},{28,16},{13,1},{17,5},{21,9},{25,13},... | collective-permute-start | bytes 147464 | tf_op jit(solution)/shard_map/ppermute | solution.py:31
  130.8 14.2 %collective-permute-start.10 = (bf16[1,64,384]{1,2,0:T(8,128)(2,1)S(1)}, bf16[1,64,384]{1,2,0:T(8,128)(2,1)S(1)}, u32[]{:S(2)}, u32[]{:S(2)}) collective-permute-start(bf16[1,64,384]{1,2,0:T(8,128)(2,1)S(1)} %constant_dynamic-update-slice_fusion.7), channel_id=1, source_target_pairs={{8,0},{12,4},{16,8},{20,12},{24,16},{28,20},{9,1},{13,5},{17,9},{2... | collective-permute-start | bytes 147464 | tf_op jit(solution)/shard_map/ppermute | solution.py:31
  132.2 12.8 %collective-permute-start.9 = (bf16[1,64,384]{1,2,0:T(8,128)(2,1)S(1)}, bf16[1,64,384]{1,2,0:T(8,128)(2,1)S(1)}, u32[]{:S(2)}, u32[]{:S(2)}) collective-permute-start(bf16[1,64,384]{1,2,0:T(8,128)(2,1)S(1)} %constant_dynamic-update-slice_fusion.7), channel_id=1, source_target_pairs={{4,0},{8,4},{12,8},{16,12},{20,16},{24,20},{28,24},{5,1},{9,5},{13... | collective-permute-start | bytes 147464 | tf_op jit(solution)/shard_map/ppermute | solution.py:31
  133.4 11.4 %collective-permute-start.8 = (bf16[1,64,384]{1,2,0:T(8,128)(2,1)S(1)}, bf16[1,64,384]{1,2,0:T(8,128)(2,1)S(1)}, u32[]{:S(2)}, u32[]{:S(2)}) collective-permute-start(bf16[1,64,384]{1,2,0:T(8,128)(2,1)S(1)} %constant_dynamic-update-slice_fusion.7), channel_id=1, source_target_pairs={{0,4},{4,8},{8,12},{12,16},{16,20},{20,24},{24,28},{1,5},{5,9},{9,... | collective-permute-start | bytes 147464 | tf_op jit(solution)/shard_map/ppermute | solution.py:31
  138.0 6.8 %collective-permute-start.7 = (bf16[1,64,384]{1,2,0:T(8,128)(2,1)S(1)}, bf16[1,64,384]{1,2,0:T(8,128)(2,1)S(1)}, u32[]{:S(2)}, u32[]{:S(2)}) collective-permute-start(bf16[1,64,384]{1,2,0:T(8,128)(2,1)S(1)} %constant_dynamic-update-slice_fusion.7), channel_id=1, source_target_pairs={{0,8},{4,12},{8,16},{12,20},{16,24},{20,28},{1,9},{5,13},{9,17},{1... | collective-permute-start | bytes 147464 | tf_op jit(solution)/shard_map/ppermute | solution.py:31
  150.5 1.0 copy-start.12
  151.5 0.8 copy-start.15
  152.4 0.8 copy-start.14
  153.2 0.8 copy-start.13
  154.9 1.0 copy-start.6
  154.9 1.0 copy-start.7
  154.9 1.0 copy-start.8
  154.9 1.1 copy-start.9
  154.9 1.1 copy-start.10
  156.1 1.4 copy-start.11
  157.4 0.7 copy-start.29
  159.8 26.9 %collective-permute-start.17 = (bf16[1,64,384]{1,2,0:T(8,128)(2,1)S(1)}, bf16[1,64,384]{1,2,0:T(8,128)(2,1)S(1)}, u32[]{:S(2)}, u32[]{:S(2)}) collective-permute-start(bf16[1,64,384]{1,2,0:T(8,128)(2,1)S(1)} %constant_dynamic-update-slice_fusion.34), channel_id=1, source_target_pairs={{12,0},{16,4},{20,8},{24,12},{28,16},{13,1},{17,5},{21,9},{25,13},... | collective-permute-start | bytes 147464 | tf_op jit(solution)/shard_map/ppermute | solution.py:31
  161.1 25.5 %collective-permute-start.16 = (bf16[1,64,384]{1,2,0:T(8,128)(2,1)S(1)}, bf16[1,64,384]{1,2,0:T(8,128)(2,1)S(1)}, u32[]{:S(2)}, u32[]{:S(2)}) collective-permute-start(bf16[1,64,384]{1,2,0:T(8,128)(2,1)S(1)} %constant_dynamic-update-slice_fusion.34), channel_id=1, source_target_pairs={{8,0},{12,4},{16,8},{20,12},{24,16},{28,20},{9,1},{13,5},{17,9},{2... | collective-permute-start | bytes 147464 | tf_op jit(solution)/shard_map/ppermute | solution.py:31
  162.4 24.2 %collective-permute-start.15 = (bf16[1,64,384]{1,2,0:T(8,128)(2,1)S(1)}, bf16[1,64,384]{1,2,0:T(8,128)(2,1)S(1)}, u32[]{:S(2)}, u32[]{:S(2)}) collective-permute-start(bf16[1,64,384]{1,2,0:T(8,128)(2,1)S(1)} %constant_dynamic-update-slice_fusion.34), channel_id=1, source_target_pairs={{4,0},{8,4},{12,8},{16,12},{20,16},{24,20},{28,24},{5,1},{9,5},{13... | collective-permute-start | bytes 147464 | tf_op jit(solution)/shard_map/ppermute | solution.py:31
  163.7 22.8 %collective-permute-start.14 = (bf16[1,64,384]{1,2,0:T(8,128)(2,1)S(1)}, bf16[1,64,384]{1,2,0:T(8,128)(2,1)S(1)}, u32[]{:S(2)}, u32[]{:S(2)}) collective-permute-start(bf16[1,64,384]{1,2,0:T(8,128)(2,1)S(1)} %constant_dynamic-update-slice_fusion.34), channel_id=1, source_target_pairs={{0,4},{4,8},{8,12},{12,16},{16,20},{20,24},{24,28},{1,5},{5,9},{9,... | collective-permute-start | bytes 147464 | tf_op jit(solution)/shard_map/ppermute | solution.py:31
  169.4 10.6 %collective-permute-start.12 = (bf16[1,64,384]{1,2,0:T(8,128)(2,1)S(1)}, bf16[1,64,384]{1,2,0:T(8,128)(2,1)S(1)}, u32[]{:S(2)}, u32[]{:S(2)}) collective-permute-start(bf16[1,64,384]{1,2,0:T(8,128)(2,1)S(1)} %constant_dynamic-update-slice_fusion.34), channel_id=1, source_target_pairs={{0,12},{4,16},{8,20},{12,24},{16,28},{1,13},{5,17},{9,21},{13,25},... | collective-permute-start | bytes 147464 | tf_op jit(solution)/shard_map/ppermute | solution.py:31
  178.2 0.7 copy-start.32
  180.0 6.5 %collective-permute-start.13 = (bf16[1,64,384]{1,2,0:T(8,128)(2,1)S(1)}, bf16[1,64,384]{1,2,0:T(8,128)(2,1)S(1)}, u32[]{:S(2)}, u32[]{:S(2)}) collective-permute-start(bf16[1,64,384]{1,2,0:T(8,128)(2,1)S(1)} %constant_dynamic-update-slice_fusion.34), channel_id=1, source_target_pairs={{0,8},{4,12},{8,16},{12,20},{16,24},{20,28},{1,9},{5,13},{9,17},{1... | collective-permute-start | bytes 147464 | tf_op jit(solution)/shard_map/ppermute | solution.py:31
  191.9 0.8 copy-start.17
  192.7 0.8 copy-start.16
  194.4 0.9 copy-start.1
  194.4 1.0 copy-start.2
  194.4 1.0 copy-start.3
  194.5 1.1 copy-start.4
  194.5 1.1 copy-start.5
  195.6 0.9 copy-start.23
  196.5 0.7 copy-start.25
  197.2 0.7 copy-start.22
  197.9 0.7 copy-start.20
Sparse Core Ops, SparseCore 0:
  178.3 125.1 all-reduce.2
where the time goes:
time: 315 us; the launch traced here: 312 us
  between operations  88.5 us (28%)
  waiting for transfers between devices  68 us (22%)
  starting transfers between devices  60.7 us (19%)
  blocking collectives  42.8 us (14%)
  local copies, waits for them, and re-layouts  41.3 us (13%)
  matrix products  6.25 us (2%)
  other arithmetic  4.71 us (1%)
    psum x1, waiting for transfers between devices, shards(): lax.psum((grad_w1, grad_b1, grad_w2, grad_b2, grad_wh, grad_bh), ('brick'...  61.9 us
    ppermute x18, starting transfers between devices, passed_along(): return lax.ppermute(block, axis, route)  60.7 us
    psum x1, blocking collectives, shards(): lax.psum((grad_w1, grad_b1, grad_w2, grad_b2, grad_wh, grad_bh), ('brick'...  42.8 us
    unnamed x121, local copies, waits for them, and re-layouts  13.5 us
    reshape x42, local copies, waits for them, and re-layouts, window_group(): views.append(padded[:, :, start_x:start_x + out_len, start_y:start_y + ou...  7.79 us
  transfers between devices with their start and end apart: 19, of which 5 were waited for; matrix products, arithmetic and copies ran while one was open for 4% of the time, Pallas kernels for 0%

commit v1 on v0

v1 whole, which is shorter than its diff:
```python
import functools
import math

import jax
import jax.numpy as jnp
from jax import lax
from jax.experimental import pallas as pl
from jax.experimental.pallas import tpu as pltpu
from jax.sharding import PartitionSpec as P

F32 = jnp.float32
BF16 = jnp.bfloat16
MESH = pl.DeviceIdType.MESH
TAPS = 27
PLANE = 64
CELLS = 512
WIDE = 640
DELTAS = (-3, -2, -1, 1, 2, 3)
CHUNKS = 8
CHUNK = 256
MAIN = 7 * CHUNK
MIC_ROWS = 32
SLOPE = math.sqrt(2 / math.pi)
CUBIC = 0.044715


def direction_id(a, c):
    full = (a + 1) * 9 + 3 + (c + 1)
    return full if full < 13 else full - 1


def iota(shape, dim):
    return lax.broadcasted_iota(jnp.int32, shape, dim)


def dot(left, right):
    return lax.dot_general(left, right, (((1,), (0,)), ((), ())), preferred_element_type=F32)


def dot_nt(left, right):
    return lax.dot_general(left, right, (((1,), (1,)), ((), ())), preferred_element_type=F32)


def column(row):
    size = row.shape[1]
    wide = jnp.broadcast_to(row, (size, size))
    return jnp.sum(jnp.where(iota((size, size), 0) == iota((size, size), 1), wide, 0.0), axis=1, keepdims=True)


def gelu_parts(values):
    square = values * values
    bent = jnp.tanh(SLOPE * (values + CUBIC * square * values))
    half = 0.5 * (1.0 + bent)
    slope = half + 0.5 * values * (1.0 - bent * bent) * (SLOPE * (1.0 + 3.0 * CUBIC * square))
    return values * half, slope


def halves(values):
    high = values.astype(BF16)
    return jnp.concatenate([high, (values - high.astype(F32)).astype(BF16)], axis=1)


def joined(pair):
    return pair[:, :128].astype(F32) + pair[:, 128:].astype(F32)


def for_each(count, body):
    if count <= 8:
        for step in range(count):
            body(step)
    else:
        def step_body(step, carry):
            body(step)
            return carry

        lax.fori_loop(0, count, step_body, 0)


def pack(field, pick, packet):
    rows = field.shape[0]
    low = iota((rows, 128), 1) < PLANE
    packet[0] = dot(field.astype(BF16), pick).astype(BF16)
    packet[1] = jnp.where(low, field[:, :128], field[:, CELLS - 128 :]).astype(BF16)


def widen(field, box, flags, spread):
    rows = field.shape[0]
    lane = iota((rows, 128), 1)
    m3, m2, m1, p1, p2, p3 = [box[k].astype(F32) for k in range(6)]
    ends = jnp.where(lane < PLANE, p2 * flags[1, 0], m2 * flags[-1, 0])
    padded = pltpu.roll(jnp.concatenate([field, ends], axis=1), 64, 1)
    first, inner, last = lane < 8, lane < 72, lane < 80
    above = jnp.where(
        first,
        pltpu.roll(m1, 72, 1) * flags[-1, 1],
        jnp.where(
            inner,
            pltpu.roll(p1, 8, 1) * flags[0, 1],
            jnp.where(last, pltpu.roll(p3, 72, 1) * flags[1, 1], 0.0),
        ),
    )
    below = jnp.where(
        first,
        pltpu.roll(m3, 8, 1) * flags[-1, -1],
        jnp.where(
            inner,
            pltpu.roll(m1, 72, 1) * flags[0, -1],
            jnp.where(last, pltpu.roll(p1, 8, 1) * flags[1, -1], 0.0),
        ),
    )
    halo = dot(jnp.concatenate([above, below], axis=1).astype(BF16), spread)
    return padded, halo


def windows(padded, halo, emit):
    lane = iota(padded.shape, 1)
    z = lane % 8
    y = (lane // 8) % 8
    for c in (-1, 0, 1):
        if c == 0:
            along = padded
        elif c == 1:
            along = jnp.where(z == 7, halo, pltpu.roll(padded, WIDE - 1, 1))
        else:
            along = jnp.where(z == 0, halo, pltpu.roll(padded, 1, 1))
        emit(3 + c + 1, along)
        emit(c + 1, jnp.where(y == 0, 0.0, pltpu.roll(along, 8, 1)))
        emit(6 + c + 1, jnp.where(y == 7, 0.0, pltpu.roll(along, WIDE - 8, 1)))


def kernel(
    nb,
    nr,
    total_bricks,
    mic_ref,
    tis_ref,
    nei_ref,
    w1_ref,
    b1_ref,
    w2_ref,
    b2_ref,
    hw_ref,
    hb_ref,
    cot_ref,
    pred_ref,
    gw1_ref,
    gb1_ref,
    gw2_ref,
    gb2_ref,
    gwh_ref,
    gbh_ref,
    s1_ref,
    s2_ref,
    w1p_ref,
    w2p_ref,
    back_ref,
    a_ref,
    pick_ref,
    spread_ref,
    mic_out,
    h1_out,
    dz_out,
    mic_box,
    h1_box,
    dz_box,
    grad_ref,
    ra_ref,
    rb_src,
    rb_ref,
    fin_ref,
    ex_send,
    ex_recv,
    a_send,
    a_recv,
    b_send,
    b_recv,
    gb_send,
    gb_recv,
    ga_send,
    ga_recv,
):
    me = lax.axis_index("brick")
    mr = lax.axis_index("region")
    channels = w2_ref.shape[0]
    rows = channels // nr

    for box in (mic_box, h1_box, dz_box):
        box[...] = jnp.zeros_like(box)

    barrier = pltpu.get_barrier_semaphore()

    def greet_brick(step):
        pl.semaphore_signal(
            barrier, inc=1, device_id={"brick": (me + 1 + step) % nb}, device_id_type=MESH
        )

    for_each(nb - 1, greet_brick)
    for step in range(nr - 1):
        pl.semaphore_signal(
            barrier, inc=1, device_id={"region": (mr + 1 + step) % nr}, device_id_type=MESH
        )

    spot, slot = iota((CELLS, 128), 0), iota((CELLS, 128), 1)
    pick_ref[...] = jnp.where(
        spot == (slot % PLANE) * 8 + 7 * (slot // PLANE), 1.0, 0.0
    ).astype(BF16)
    pick = pick_ref[...]
    mic = jnp.broadcast_to(mic_ref[...].astype(F32), (MIC_ROWS, CELLS))
    pack(mic, pick, mic_out)

    def exchange(index, packet, box, act):
        for k, delta in enumerate(DELTAS):
            back = DELTAS.index(-delta)
            other = me + delta

            @pl.when((other >= 0) & (other < nb))
            def _():
                if act == "recv":
                    copy = pltpu.make_async_remote_copy(
                        src_ref=packet.at[1 if abs(delta) == 2 else 0],
                        dst_ref=box.at[k],
                        send_sem=ex_send.at[index, k],
                        recv_sem=ex_recv.at[index, k],
                        device_id={"brick": other},
                        device_id_type=MESH,
                    )
                    copy.wait_recv()
                else:
                    copy = pltpu.make_async_remote_copy(
                        src_ref=packet.at[1 if abs(delta) == 2 else 0],
                        dst_ref=box.at[back],
                        send_sem=ex_send.at[index, k],
                        recv_sem=ex_recv.at[index, back],
                        device_id={"brick": other},
                        device_id_type=MESH,
                    )
                    if act == "start":
                        copy.start()
                    else:
                        copy.wait_send()

    pl.semaphore_wait(barrier, nb - 1 + nr - 1)
    exchange(0, mic_out, mic_box, "start")

    spread_row, spread_lane = iota((256, WIDE), 0), iota((256, WIDE), 1)
    spread_ref[...] = jnp.where(
        spread_lane == (spread_row % 128) * 8 + 7 * (1 - spread_row // 128), 1.0, 0.0
    ).astype(BF16)
    w1p_ref[...] = jnp.zeros_like(w1p_ref)
    w1p_ref[:, :TAPS] = w1_ref[...]
    w2p_ref[:, MAIN - 128 :] = jnp.zeros((channels, 128), BF16)
    w2p_ref[:, : TAPS * channels] = w2_ref[...]
    s1_ref[TAPS * channels :, :] = jnp.zeros((channels, CELLS), BF16)
    s2_ref[TAPS * channels :, :] = jnp.zeros((channels, CELLS), BF16)
    for j in range(14):
        upper = w2p_ref[:, 128 * (13 - j) : 128 * (14 - j)].astype(F32)
        if j < 13:
            lower = w2p_ref[:, 128 * (12 - j) : 128 * (13 - j)].astype(F32)
        else:
            lower = jnp.zeros((channels, 128), F32)
        turned = jnp.concatenate([upper, lower], axis=0).T
        back_ref[:, 128 * j : 128 * (j + 1)] = jnp.where(
            iota((channels, 128), 1) < channels, turned[:channels], turned[channels:]
        ).astype(BF16)
    flags = {}
    for a in (-1, 0, 1):
        for c in (-1, 0, 1):
            if (a, c) != (0, 0):
                flags[a, c] = jnp.where(nei_ref[0, direction_id(a, c)] >= 0, 1.0, 0.0).astype(F32)
    active = tis_ref[0, 0].astype(F32)
    bias1 = column(b1_ref[...])
    bias2 = column(b2_ref[...])
    bias3 = jnp.sum(
        jnp.where(iota((4, 4), 0) == iota((4, 4), 1), jnp.broadcast_to(hb_ref[...], (4, 4)), 0.0),
        axis=1,
        keepdims=True,
    )
    dpred = (cot_ref[...].astype(F32) * active / total_bricks).astype(BF16)
    dpred_wide = jnp.concatenate([dpred.astype(F32), jnp.zeros((4, CELLS), F32)], axis=0)
    d_second = lax.dot_general(
        hw_ref[...], dpred, (((0,), (0,)), ((), ())), preferred_element_type=F32
    )

    exchange(0, mic_out, mic_box, "recv")
    spread = spread_ref[...]
    padded, halo = widen(mic, mic_box, flags, spread)
    row = iota((MIC_ROWS, CELLS), 0)
    taps = [jnp.where((row >= 27) & (row < 30), 1.0, 0.0).astype(F32)]

    def emit_mic(index, value):
        rolled = pltpu.roll(value, WIDE - PLANE, 1)
        views = (value[:, :CELLS], rolled[:, :CELLS], value[:, 128:])
        for a in range(3):
            taps[0] = jnp.where(row == 9 * a + index, views[a], taps[0])

    windows(padded, halo, emit_mic)
    a_ref[...] = jnp.concatenate(
        [taps[0], dpred_wide, jnp.zeros((128 - MIC_ROWS - 8, CELLS), F32)], axis=0
    ).astype(BF16)
    z1 = dot(w1p_ref[...], a_ref[...]) + bias1
    value1, slope1 = gelu_parts(z1)
    h1 = (value1 * active).astype(BF16).astype(F32)
    pack(h1, pick, h1_out)
    exchange(1, h1_out, h1_box, "start")
    slope1 = slope1 * active

    def store_windows(target):
        def emit(index, value):
            rolled = pltpu.roll(value, WIDE - PLANE, 1)
            views = (value[:, :CELLS], rolled[:, :CELLS], value[:, 128:])
            for a in range(3):
                start = (9 * a + index) * channels
                target[start : start + channels, :] = views[a].astype(BF16)

        return emit

    exchange(1, h1_out, h1_box, "recv")
    padded, halo = widen(h1, h1_box, flags, spread)
    windows(padded, halo, store_windows(s1_ref))
    z2 = dot(w2p_ref[...], s1_ref[...]) + bias2
    value2, slope2 = gelu_parts(z2)
    dz2 = (d_second * slope2 * active).astype(BF16)
    pack(dz2.astype(F32), pick, dz_out)
    exchange(2, dz_out, dz_box, "start")

    grad_ref[:, :MAIN] = dot_nt(dz2, s1_ref[...]).astype(BF16)

    def region_copy(part, step, act):
        other = (mr + 1 + step) % nr
        lanes = pl.ds(0, MAIN) if part == 0 else pl.ds(MAIN, CHUNK)
        owner = other if act != "recv" else mr
        slot_id = mr if act != "recv" else other
        copy = pltpu.make_async_remote_copy(
            src_ref=grad_ref.at[pl.ds(pl.multiple_of(owner * rows, rows), rows), lanes],
            dst_ref=ra_ref.at[slot_id, :, lanes],
            send_sem=a_send.at[part, other],
            recv_sem=a_recv.at[part, slot_id],
            device_id={"region": other},
            device_id_type=MESH,
        )
        if act == "start":
            copy.start()
        elif act == "recv":
            copy.wait_recv()
        else:
            copy.wait_send()

    for step in range(nr - 1):
        region_copy(0, step, "start")

    h2 = (value2 * active).astype(BF16)
    linear = dot(hw_ref[...], h2) + bias3
    pred_ref[...] = (linear * active).astype(BF16)
    tap_rows = a_ref[...]
    dpred_tall = jnp.concatenate(
        [dpred_wide, jnp.zeros((channels - 8, CELLS), F32)], axis=0
    ).astype(BF16)
    lane = iota((channels, 128), 1)
    small = jnp.where(lane == 28, dot_nt(dz2, tap_rows), 0.0)
    small = small + jnp.where((lane >= 32) & (lane < 36), dot_nt(h2, tap_rows), 0.0)
    small = small + jnp.where(lane == 29, dot_nt(dpred_tall, tap_rows), 0.0)

    exchange(2, dz_out, dz_box, "recv")
    padded, halo = widen(dz2.astype(F32), dz_box, flags, spread)
    windows(padded, halo, store_windows(s2_ref))
    dz1 = (dot(back_ref[...], s2_ref[...]) * slope1).astype(BF16)
    small = small + jnp.where(lane < 28, dot_nt(dz1, tap_rows), 0.0)
    grad_ref[:, MAIN:] = halves(small)
    for step in range(nr - 1):
        region_copy(1, step, "start")

    def brick_copy(chunk, act):
        @pl.when(me != chunk)
        def _():
            copy = pltpu.make_async_remote_copy(
                src_ref=rb_src.at[chunk],
                dst_ref=rb_ref.at[me],
                send_sem=b_send.at[chunk],
                recv_sem=b_recv.at[me],
                device_id={"brick": chunk},
                device_id_type=MESH,
            )
            if act == "start":
                copy.start()
            else:
                copy.wait_send()

    mine = pl.ds(pl.multiple_of(mr * rows, rows), rows)

    def region_sum(part):
        lanes = pl.ds(0, MAIN) if part == 0 else pl.ds(MAIN, CHUNK)
        for step in range(nr - 1):
            region_copy(part, step, "recv")
        total = grad_ref[mine, lanes].astype(F32)
        for step in range(nr - 1):
            total = total + ra_ref[(mr + 1 + step) % nr, :, lanes].astype(F32)
        return total

    total = region_sum(0)
    for chunk in range(CHUNKS - 1):
        rb_src[chunk] = total[:, CHUNK * chunk : CHUNK * (chunk + 1)].astype(BF16)
        brick_copy(chunk, "start")
    rb_src[CHUNKS - 1] = halves(joined(region_sum(1)))
    brick_copy(CHUNKS - 1, "start")

    def gather_copy(step, act):
        other = (me + 1 + step) % nb
        copy = pltpu.make_async_remote_copy(
            src_ref=fin_ref.at[mr, me % CHUNKS],
            dst_ref=fin_ref.at[mr, me % CHUNKS],
            send_sem=gb_send.at[other],
            recv_sem=gb_recv.at[me % CHUNKS],
            device_id={"brick": other},
            device_id_type=MESH,
        )
        if act == "start":
            copy.start()
        else:
            copy.wait_send()

    def own():
        def arrived(step):
            other = (me + 1 + step) % nb
            pltpu.make_async_remote_copy(
                src_ref=rb_src.at[0],
                dst_ref=rb_ref.at[other],
                send_sem=b_send.at[0],
                recv_sem=b_recv.at[other],
                device_id={"brick": other},
                device_id_type=MESH,
            ).wait_recv()

        for_each(nb - 1, arrived)
        kept = rb_src[me % CHUNKS].astype(F32)
        if nb <= CHUNKS:
            for step in range(nb - 1):
                kept = kept + rb_ref[(me + 1 + step) % nb].astype(F32)
        else:
            kept = lax.fori_loop(
                0, nb - 1, lambda step, s: s + rb_ref[(me + 1 + step) % nb].astype(F32), kept
            )
        fin_ref[mr, me % CHUNKS] = jnp.where(me == CHUNKS - 1, halves(joined(kept)), kept.astype(BF16))
        for_each(nb - 1, lambda step: gather_copy(step, "start"))

    if nb > CHUNKS:
        pl.when(me < CHUNKS)(own)
    else:
        own()

    for chunk in range(CHUNKS):
        @pl.when(me != chunk)
        def _():
            pltpu.make_async_remote_copy(
                src_ref=fin_ref.at[mr, chunk],
                dst_ref=fin_ref.at[mr, chunk],
                send_sem=gb_send.at[chunk],
                recv_sem=gb_recv.at[chunk],
                device_id={"brick": chunk},
                device_id_type=MESH,
            ).wait_recv()

    def spread_copy(step, act):
        other = (mr + 1 + step) % nr
        slot_id = other if act == "recv" else mr
        copy = pltpu.make_async_remote_copy(
            src_ref=fin_ref.at[slot_id],
            dst_ref=fin_ref.at[slot_id],
            send_sem=ga_send.at[other],
            recv_sem=ga_recv.at[slot_id],
            device_id={"region": other},
            device_id_type=MESH,
        )
        if act == "start":
            copy.start()
        elif act == "recv":
            copy.wait_recv()
        else:
            copy.wait_send()

    for step in range(nr - 1):
        spread_copy(step, "start")
    exchange(0, mic_out, mic_box, "sent")
    exchange(1, h1_out, h1_box, "sent")
    exchange(2, dz_out, dz_box, "sent")
    for part in range(2):
        for step in range(nr - 1):
            region_copy(part, step, "sent")
    for chunk in range(CHUNKS):
        brick_copy(chunk, "sent")
    if nb > CHUNKS:
        pl.when(me < CHUNKS)(lambda: for_each(nb - 1, lambda step: gather_copy(step, "sent")))
    else:
        for_each(nb - 1, lambda step: gather_copy(step, "sent"))
    for step in range(nr - 1):
        spread_copy(step, "recv")
    for region in range(nr):
        where = slice(region * rows, (region + 1) * rows)
        for chunk in range(CHUNKS - 1):
            block = fin_ref[region, chunk].astype(F32)
            if chunk < CHUNKS - 2:
                gw2_ref[where, CHUNK * chunk : CHUNK * (chunk + 1)] = block
            else:
                gw2_ref[where, CHUNK * chunk : CHUNK * chunk + 128] = block[:, :128]
                gw2_ref[where, CHUNK * chunk + 128 : TAPS * channels] = block[
                    :, 128 : TAPS * channels - CHUNK * chunk
                ]
    small = jnp.concatenate(
        [joined(fin_ref[region, CHUNKS - 1]) for region in range(nr)], axis=0
    )
    gw1_ref[...] = small[:, :TAPS]
    turned = jnp.concatenate([small, jnp.zeros((128 - channels, 128), F32)], axis=0).T
    gb1_ref[...] = turned[27:28, :channels]
    gb2_ref[...] = turned[28:29, :channels]
    gbh_ref[...] = turned[29:30, :4]
    gwh_ref[...] = turned[32:36, :channels]
    for step in range(nr - 1):
        spread_copy(step, "sent")


def solution(mesh):
    nb, nr = mesh.shape["brick"], mesh.shape["region"]

    def shards(mic, tissue, neighbours, w1, b1, w2, b2, hw, hb, cot):
        channels = w1.shape[0]
        rows = channels // nr
        vmem = pl.BlockSpec(memory_space=pltpu.VMEM)
        smem = pl.BlockSpec(memory_space=pltpu.SMEM)
        dma = pltpu.SemaphoreType.DMA
        total_bricks = nb * nr * mic.shape[1]
        outs = pl.pallas_call(
            functools.partial(kernel, nb, nr, total_bricks),
            out_shape=(
                jax.ShapeDtypeStruct((4, CELLS), BF16),
                jax.ShapeDtypeStruct((channels, TAPS), F32),
                jax.ShapeDtypeStruct((1, channels), F32),
                jax.ShapeDtypeStruct((channels, TAPS * channels), F32),
                jax.ShapeDtypeStruct((1, channels), F32),
                jax.ShapeDtypeStruct((4, channels), F32),
                jax.ShapeDtypeStruct((1, 4), F32),
            ),
            in_specs=[vmem, smem, smem] + [vmem] * 7,
            out_specs=(vmem,) * 7,
            scratch_shapes=[
                pltpu.VMEM((MAIN, CELLS), BF16),
                pltpu.VMEM((MAIN, CELLS), BF16),
                pltpu.VMEM((channels, 128), BF16),
                pltpu.VMEM((channels, MAIN), BF16),
                pltpu.VMEM((channels, MAIN), BF16),
                pltpu.VMEM((128, CELLS), BF16),
                pltpu.VMEM((CELLS, 128), BF16),
                pltpu.VMEM((256, WIDE), BF16),
                pltpu.VMEM((2, MIC_ROWS, 128), BF16),
                pltpu.VMEM((2, channels, 128), BF16),
                pltpu.VMEM((2, channels, 128), BF16),
                pltpu.VMEM((6, MIC_ROWS, 128), BF16),
                pltpu.VMEM((6, channels, 128), BF16),
                pltpu.VMEM((6, channels, 128), BF16),
                pltpu.VMEM((channels, MAIN + CHUNK), BF16),
                pltpu.VMEM((nr, rows, MAIN + CHUNK), BF16),
                pltpu.VMEM((CHUNKS, rows, CHUNK), BF16),
                pltpu.VMEM((nb, rows, CHUNK), BF16),
                pltpu.VMEM((nr, CHUNKS, rows, CHUNK), BF16),
                dma((3, 6)),
                dma((3, 6)),
                dma((2, nr)),
                dma((2, nr)),
                dma((CHUNKS,)),
                dma((nb,)),
                dma((nb,)),
                dma((CHUNKS,)),
                dma((nr,)),
                dma((nr,)),
            ],
            compiler_params=pltpu.CompilerParams(
                collective_id=0, has_side_effects=True, vmem_limit_bytes=40 * 1024 * 1024
            ),
            cost_estimate=pl.CostEstimate(flops=360_000_000, bytes_accessed=2_000_000, transcendentals=65536),
        )(
            mic.reshape(1, CELLS),
            tissue,
            neighbours.reshape(1, 26),
            w1,
            b1.reshape(1, channels),
            w2,
            b2.reshape(1, channels),
            hw,
            hb.reshape(1, 4),
            cot.reshape(4, CELLS),
        )
        pred, gw1, gb1, gw2, gb2, gwh, gbh = outs
        return (
            pred.reshape(1, 1, 4, CELLS),
            gw1,
            gb1.reshape(channels),
            gw2,
            gb2.reshape(channels),
            gwh,
            gbh.reshape(4),
        )

    return jax.shard_map(
        shards,
        mesh=mesh,
        in_specs=(
            P("region", "brick", None),
            P("region", "brick"),
            P("region", "brick", None),
            P(),
            P(),
            P(),
            P(),
            P(),
            P(),
            P("region", "brick", None, None),
        ),
        out_specs=(P("region", "brick", None, None), P(), P(), P(), P(), P(), P()),
        check_vma=False,
    )
```

time: 315 us -> 42.2 us (0.13)
  between operations: 88.5 us -> 1.36 us
  waiting for transfers between devices: 68 us -> 0 us
  starting transfers between devices: 60.7 us -> 0 us
  blocking collectives: 42.8 us -> 0 us
  local copies, waits for them, and re-layouts: 41.3 us -> 5.83 us
  Pallas kernels: 0 us -> 34.7 us
  matrix products: 6.25 us -> 0 us
  other arithmetic: 4.71 us -> 0 us
    psum x1 -> x0, waiting for transfers between devices: 61.9 us -> none  [shards(): lax.psum((grad_w1, grad_b1, grad_w2, grad_b2, grad_wh, grad_bh), ('brick'...]
    ppermute x18 -> x0, starting transfers between devices: 60.7 us -> none  [passed_along(): return lax.ppermute(block, axis, route)]
    psum x1 -> x0, blocking collectives: 42.8 us -> none  [shards(): lax.psum((grad_w1, grad_b1, grad_w2, grad_b2, grad_wh, grad_bh), ('brick'...]
    pallas_call x0 -> x1, Pallas kernels: none -> 34.7 us  [shards(): pl.pallas_call(functools.partial(kernel, nb, nr, total_bricks), out_shape...]
    slice x32 -> x0, local copies, waits for them, and re-layouts: 10.9 us -> none  [the longest x8 4.69 us: assemble(): portion = selected[:, :, sources[0], sources[1], sources[2]]]
    reshape x69 -> x0, local copies, waits for them, and re-layouts: 10.5 us -> none  [the longest x42 7.79 us: window_group(): views.append(padded[:, :, start_x:start_x + out_len, start_y:start_y + ou...]
    unnamed x121 -> x26, local copies, waits for them, and re-layouts: 13.5 us -> 5.83 us
    dot_general x18 -> x0, matrix products: 6.25 us -> none  [the longest x9 3.92 us: convolve(): jnp.einsum('oj,njp->nop', grouped, stacked, preferred_element_type=jnp.fl...]
  transfers between devices with their start and end apart: 19 -> 0, of which waited for: 5 -> 0; matrix products, arithmetic and copies ran while one was open for 4% -> 0% of each run, Pallas kernels for 0% -> 0%
where the time goes in v1:
time: 42.2 us; the launch traced here: 41.8 us
  Pallas kernels  34.7 us (82%)
  local copies, waits for them, and re-layouts  5.83 us (14%)
  between operations  1.36 us (3%)
    pallas_call x1, Pallas kernels, shards(): pl.pallas_call(functools.partial(kernel, nb, nr, total_bricks), out_shape...  34.7 us
    unnamed x26, local copies, waits for them, and re-layouts  5.83 us

profile of v1, /device:TPU:0, one launch (start us, length us, event | category | flops | bytes accessed | tf_op | source)
XLA Modules:
  0.0 41.8 jit_solution(8547940923607304657)
XLA Ops:
  0.6 0.0 copy-start.8
  1.3 0.0 copy-done.8
  1.3 0.0 copy-start.1
  1.3 0.0 copy-start.2
  1.3 0.0 copy-start.3
  1.3 0.0 copy-start.4
  1.4 0.0 copy-start.5
  1.4 0.0 copy-start.6
  1.4 0.0 copy-start.7
  1.4 0.1 copy.17.w1_ref
  1.5 0.5 %copy-done.1 = bf16[1,1,4,512]{3,2,1,0:T(4,128)(2,1)S(1)} copy-done((bf16[1,1,4,512]{3,2,1,0:T(4,128)(2,1)S(1)}, bf16[1,1,4,512]{3,2,1,0:T(4,128)(2,1)}, u32[]{:S(2)}) %copy-start.1) | copy-done | bytes 4120
  2.0 0.0 copy-done.2
  2.0 0.0 copy-done.3
  2.0 0.0 copy-done.4
  2.0 0.0 copy-done.5
  2.1 0.0 copy-done.6
  2.1 0.0 copy-done.7
  2.1 0.0 copy-start
  2.1 0.9 %copy-done = bf16[64,1728]{1,0:T(8,128)(2,1)S(1)} copy-done((bf16[64,1728]{1,0:T(8,128)(2,1)S(1)}, bf16[64,1728]{1,0:T(8,128)(2,1)}, u32[]{:S(2)}) %copy-start) | copy-done | bytes 221208
  3.0 34.7 %shard_map.153 = (bf16[4,512]{1,0:T(4,128)(2,1)S(1)}, f32[64,27]{1,0:T(8,128)S(1)}, f32[1,64]{1,0:T(1,128)S(1)}, f32[64,1728]{1,0:T(8,128)S(1)}, f32[1,64]{1,0:T...) custom-call(bf16[1,512]{1,0:T(2,128)(2,1)S(1)} %bitcast.12, s32[1,1]{1,0:T(1,128)S(6)} %copy.25.tis_ref, ...), custom_call_target="tpu_custom_call" | custom-call | flops 360000000 | bytes 2000000 | tf_op jit(solution)/shard_map/pallas_call | solution.py:530
  37.7 0.7 %copy.18 = f32[64,27]{0,1:T(8,128)} copy(f32[64,27]{1,0:T(8,128)S(1)} %get-tuple-element.22) | data formatting | bytes 13824
  38.4 0.6 %copy.26 = bf16[1,1,4,512]{3,2,1,0:T(4,128)(2,1)} copy(bf16[1,1,4,512]{3,2,1,0:T(4,128)(2,1)S(1)} %bitcast.10) | data formatting | bytes 8192
  39.0 0.5 %copy.27 = f32[64]{0:T(128)} copy(f32[64]{0:T(128)S(1)} %bitcast.19) | data formatting | bytes 512
  39.5 0.8 %copy.28 = f32[64,1728]{1,0:T(8,128)} copy(f32[64,1728]{1,0:T(8,128)S(1)} %get-tuple-element.38) | data formatting | bytes 884736
  40.2 0.5 %copy.29 = f32[64]{0:T(128)} copy(f32[64]{0:T(128)S(1)} %bitcast.18) | data formatting | bytes 512
  40.8 0.6 %copy.30 = f32[4,64]{1,0:T(4,128)} copy(f32[4,64]{1,0:T(4,128)S(1)} %get-tuple-element.40) | data formatting | bytes 2048
  41.3 0.5 %copy.31 = f32[4]{0:T(128)} copy(f32[4]{0:T(128)S(1)} %bitcast.17) | data formatting | bytes 32
Async XLA Ops:
  0.6 0.7 %copy-start.8 = (bf16[64,27]{0,1:T(8,128)(2,1)S(1)}, bf16[64,27]{0,1:T(8,128)(2,1)}, u32[]{:S(2)}) copy-start(bf16[64,27]{0,1:T(8,128)(2,1)} %param.13) | copy-start | bytes 10372
  1.3 0.7 %copy-start.1 = (bf16[1,1,4,512]{3,2,1,0:T(4,128)(2,1)S(1)}, bf16[1,1,4,512]{3,2,1,0:T(4,128)(2,1)}, u32[]{:S(2)}) copy-start(bf16[1,1,4,512]{3,2,1,0:T(4,128)(2,1)} %param.19) | copy-start | bytes 12292
  1.3 0.7 %copy-start.2 = (bf16[1,1,512]{2,1,0:T(2,128)(2,1)S(1)}, bf16[1,1,512]{2,1,0:T(2,128)(2,1)}, u32[]{:S(2)}) copy-start(bf16[1,1,512]{2,1,0:T(2,128)(2,1)} %param.10) | copy-start | bytes 3076
  1.3 0.7 %copy-start.3 = (bf16[4,64]{1,0:T(4,128)(2,1)S(1)}, bf16[4,64]{1,0:T(4,128)(2,1)}, u32[]{:S(2)}) copy-start(bf16[4,64]{1,0:T(4,128)(2,1)} %hw_ref.1) | copy-start | bytes 1540
  1.3 0.7 %copy-start.4 = (s32[1,1,26]{2,1,0:T(1,128)S(1)}, s32[1,1,26]{2,1,0:T(1,128)}, u32[]{:S(2)}) copy-start(s32[1,1,26]{2,1,0:T(1,128)} %param.12) | copy-start | bytes 316
  1.4 0.7 %copy-start.5 = (f32[64]{0:T(128)S(1)}, f32[64]{0:T(128)}, u32[]{:S(2)}) copy-start(f32[64]{0:T(128)} %param.14) | copy-start | bytes 772
  1.4 0.7 %copy-start.6 = (f32[64]{0:T(128)S(1)}, f32[64]{0:T(128)}, u32[]{:S(2)}) copy-start(f32[64]{0:T(128)} %param.16) | copy-start | bytes 772
  1.4 0.7 %copy-start.7 = (f32[4]{0:T(128)S(1)}, f32[4]{0:T(128)}, u32[]{:S(2)}) copy-start(f32[4]{0:T(128)} %param.18) | copy-start | bytes 52
  2.1 0.9 %copy-start = (bf16[64,1728]{1,0:T(8,128)(2,1)S(1)}, bf16[64,1728]{1,0:T(8,128)(2,1)}, u32[]{:S(2)}) copy-start(bf16[64,1728]{1,0:T(8,128)(2,1)} %w2_ref.1) | copy-start | bytes 663556

commit v2 on v1

--- a/solution.py
+++ b/solution.py
@@ -143,16 +143,12 @@
     hb_ref,
     cot_ref,
     pred_ref,
-    gw1_ref,
-    gb1_ref,
-    gw2_ref,
-    gb2_ref,
-    gwh_ref,
-    gbh_ref,
+    fin_ref,
     s1_ref,
     s2_ref,
     w1p_ref,
     w2p_ref,
+    front_ref,
     back_ref,
     a_ref,
     pick_ref,
@@ -167,7 +163,8 @@
     ra_ref,
     rb_src,
     rb_ref,
-    fin_ref,
+    w2_box,
+    w2_sem,
     ex_send,
     ex_recv,
     a_send,
@@ -184,6 +181,8 @@
     channels = w2_ref.shape[0]
     rows = channels // nr
 
+    fetch = pltpu.make_async_copy(w2_ref, w2_box, w2_sem)
+    fetch.start()
     for box in (mic_box, h1_box, dz_box):
         box[...] = jnp.zeros_like(box)
 
@@ -247,21 +246,19 @@
         spread_lane == (spread_row % 128) * 8 + 7 * (1 - spread_row // 128), 1.0, 0.0
     ).astype(BF16)
     w1p_ref[...] = jnp.zeros_like(w1p_ref)
-    w1p_ref[:, :TAPS] = w1_ref[...]
+    w1p_ref[:TAPS, :] = w1_ref[...]
+    s1_ref[9 * channels :, :] = jnp.zeros((channels, WIDE), BF16)
+    s2_ref[9 * channels :, :] = jnp.zeros((channels, WIDE), BF16)
+    fetch.wait()
     w2p_ref[:, MAIN - 128 :] = jnp.zeros((channels, 128), BF16)
-    w2p_ref[:, : TAPS * channels] = w2_ref[...]
-    s1_ref[TAPS * channels :, :] = jnp.zeros((channels, CELLS), BF16)
-    s2_ref[TAPS * channels :, :] = jnp.zeros((channels, CELLS), BF16)
-    for j in range(14):
-        upper = w2p_ref[:, 128 * (13 - j) : 128 * (14 - j)].astype(F32)
-        if j < 13:
-            lower = w2p_ref[:, 128 * (12 - j) : 128 * (13 - j)].astype(F32)
-        else:
-            lower = jnp.zeros((channels, 128), F32)
-        turned = jnp.concatenate([upper, lower], axis=0).T
-        back_ref[:, 128 * j : 128 * (j + 1)] = jnp.where(
-            iota((channels, 128), 1) < channels, turned[:channels], turned[channels:]
-        ).astype(BF16)
+    w2p_ref[:, : TAPS * channels] = w2_box[...]
+    taps_lane = iota((channels, WIDE), 1) < 9 * channels
+    for a in range(3):
+        view = w2p_ref[:, 512 * a + 64 * a - 64 * (a % 2) : 512 * a + 64 * a - 64 * (a % 2) + WIDE]
+        if a % 2:
+            view = pltpu.roll(view.astype(F32), WIDE - 64, 1)
+        view = jnp.where(taps_lane, view.astype(F32), 0.0)
+        front_ref[a * channels : (a + 1) * channels, :] = view.astype(BF16)
     flags = {}
     for a in (-1, 0, 1):
         for c in (-1, 0, 1):
@@ -297,33 +294,73 @@
     a_ref[...] = jnp.concatenate(
         [taps[0], dpred_wide, jnp.zeros((128 - MIC_ROWS - 8, CELLS), F32)], axis=0
     ).astype(BF16)
-    z1 = dot(w1p_ref[...], a_ref[...]) + bias1
+    z1 = (
+        lax.dot_general(
+            w1p_ref[...], a_ref[...], (((0,), (0,)), ((), ())), preferred_element_type=F32
+        )
+        + bias1
+    )
     value1, slope1 = gelu_parts(z1)
     h1 = (value1 * active).astype(BF16).astype(F32)
     pack(h1, pick, h1_out)
     exchange(1, h1_out, h1_box, "start")
     slope1 = slope1 * active
 
+    back = []
+    for j in range(14):
+        upper = w2p_ref[:, 128 * (13 - j) : 128 * (14 - j)].astype(F32)
+        if j == 0:
+            upper = jnp.where(iota((channels, 128), 1) < channels, upper, 0.0)
+        if j < 13:
+            lower = w2p_ref[:, 128 * (12 - j) : 128 * (13 - j)].astype(F32)
+        else:
+            lower = jnp.zeros((channels, 128), F32)
+        turned = jnp.concatenate([upper, lower], axis=0).T
+        back.append(
+            jnp.where(iota((channels, 128), 1) < channels, turned[:channels], turned[channels:])
+        )
+    for a in range(3):
+        first_tile = (9 * a) // 2
+        view = jnp.concatenate(back[first_tile : first_tile + 5], axis=1)
+        if a % 2:
+            view = pltpu.roll(view, WIDE - 64, 1)
+        view = jnp.where(taps_lane, view, 0.0)
+        back_ref[a * channels : (a + 1) * channels, :] = view.astype(BF16)
+
     def store_windows(target):
         def emit(index, value):
-            rolled = pltpu.roll(value, WIDE - PLANE, 1)
-            views = (value[:, :CELLS], rolled[:, :CELLS], value[:, 128:])
-            for a in range(3):
-                start = (9 * a + index) * channels
-                target[start : start + channels, :] = views[a].astype(BF16)
+            target[index * channels : (index + 1) * channels, :] = value.astype(BF16)
 
         return emit
+
+    def convolve(weights, target):
+        wide = dot(weights[...], target[...])
+        middle = pltpu.roll(wide[channels : 2 * channels], WIDE - PLANE, 1)
+        return (
+            wide[:channels, :CELLS] + middle[:, :CELLS] + wide[2 * channels :, WIDE - CELLS :]
+        )
 
     exchange(1, h1_out, h1_box, "recv")
     padded, halo = widen(h1, h1_box, flags, spread)
     windows(padded, halo, store_windows(s1_ref))
-    z2 = dot(w2p_ref[...], s1_ref[...]) + bias2
+    z2 = convolve(front_ref, s1_ref) + bias2
     value2, slope2 = gelu_parts(z2)
     dz2 = (d_second * slope2 * active).astype(BF16)
     pack(dz2.astype(F32), pick, dz_out)
     exchange(2, dz_out, dz_box, "start")
 
-    grad_ref[:, :MAIN] = dot_nt(dz2, s1_ref[...]).astype(BF16)
+    dz2_wide = dz2.astype(F32)
+    gap = jnp.zeros((channels, 128), F32)
+    left = jnp.concatenate([dz2_wide, gap], axis=1)
+    stacked = jnp.concatenate(
+        [left, pltpu.roll(left, PLANE, 1), jnp.concatenate([gap, dz2_wide], axis=1)], axis=0
+    ).astype(BF16)
+    grads = dot_nt(stacked, s1_ref[...])
+    centre = pltpu.roll(grads[channels : 2 * channels], PLANE, 1)
+    grad_ref[:, :512] = grads[:channels, :512].astype(BF16)
+    grad_ref[:, 512:640] = (grads[:channels, 512:] + centre[:, :128]).astype(BF16)
+    grad_ref[:, 640:1152] = centre[:, 128:].astype(BF16)
+    grad_ref[:, 1152:MAIN] = grads[2 * channels :].astype(BF16)
 
     def region_copy(part, step, act):
         other = (mr + 1 + step) % nr
@@ -359,15 +396,6 @@
     small = jnp.where(lane == 28, dot_nt(dz2, tap_rows), 0.0)
     small = small + jnp.where((lane >= 32) & (lane < 36), dot_nt(h2, tap_rows), 0.0)
     small = small + jnp.where(lane == 29, dot_nt(dpred_tall, tap_rows), 0.0)
-
-    exchange(2, dz_out, dz_box, "recv")
-    padded, halo = widen(dz2.astype(F32), dz_box, flags, spread)
-    windows(padded, halo, store_windows(s2_ref))
-    dz1 = (dot(back_ref[...], s2_ref[...]) * slope1).astype(BF16)
-    small = small + jnp.where(lane < 28, dot_nt(dz1, tap_rows), 0.0)
-    grad_ref[:, MAIN:] = halves(small)
-    for step in range(nr - 1):
-        region_copy(1, step, "start")
 
     def brick_copy(chunk, act):
         @pl.when(me != chunk)
@@ -396,12 +424,18 @@
             total = total + ra_ref[(mr + 1 + step) % nr, :, lanes].astype(F32)
         return total
 
+    exchange(2, dz_out, dz_box, "recv")
+    padded, halo = widen(dz2.astype(F32), dz_box, flags, spread)
+    windows(padded, halo, store_windows(s2_ref))
     total = region_sum(0)
     for chunk in range(CHUNKS - 1):
         rb_src[chunk] = total[:, CHUNK * chunk : CHUNK * (chunk + 1)].astype(BF16)
         brick_copy(chunk, "start")
-    rb_src[CHUNKS - 1] = halves(joined(region_sum(1)))
-    brick_copy(CHUNKS - 1, "start")
+    dz1 = (convolve(back_ref, s2_ref) * slope1).astype(BF16)
+    small = small + jnp.where(lane < 28, dot_nt(dz1, tap_rows), 0.0)
+    grad_ref[:, MAIN:] = halves(small)
+    for step in range(nr - 1):
+        region_copy(1, step, "start")
 
     def gather_copy(step, act):
         other = (me + 1 + step) % nb
@@ -418,7 +452,7 @@
         else:
             copy.wait_send()
 
-    def own():
+    def own(final):
         def arrived(step):
             other = (me + 1 + step) % nb
             pltpu.make_async_remote_copy(
@@ -439,13 +473,31 @@
             kept = lax.fori_loop(
                 0, nb - 1, lambda step, s: s + rb_ref[(me + 1 + step) % nb].astype(F32), kept
             )
-        fin_ref[mr, me % CHUNKS] = jnp.where(me == CHUNKS - 1, halves(joined(kept)), kept.astype(BF16))
+        fin_ref[mr, me % CHUNKS] = halves(joined(kept)) if final else kept.astype(BF16)
         for_each(nb - 1, lambda step: gather_copy(step, "start"))
 
-    if nb > CHUNKS:
-        pl.when(me < CHUNKS)(own)
-    else:
-        own()
+    def spread_copy(chunk, step, act):
+        other = (mr + 1 + step) % nr
+        slot_id = other if act == "recv" else mr
+        copy = pltpu.make_async_remote_copy(
+            src_ref=fin_ref.at[slot_id, chunk],
+            dst_ref=fin_ref.at[slot_id, chunk],
+            send_sem=ga_send.at[other, chunk],
+            recv_sem=ga_recv.at[slot_id, chunk],
+            device_id={"region": other},
+            device_id_type=MESH,
+        )
+        if act == "start":
+            copy.start()
+        elif act == "recv":
+            copy.wait_recv()
+        else:
+            copy.wait_send()
+
+    pl.when(me < CHUNKS - 1)(lambda: own(False))
+    rb_src[CHUNKS - 1] = halves(joined(region_sum(1)))
+    brick_copy(CHUNKS - 1, "start")
+    pl.when(me == CHUNKS - 1)(lambda: own(True))
 
     for chunk in range(CHUNKS):
         @pl.when(me != chunk)
@@ -459,26 +511,9 @@
                 device_id_type=MESH,
             ).wait_recv()
 
-    def spread_copy(step, act):
-        other = (mr + 1 + step) % nr
-        slot_id = other if act == "recv" else mr
-        copy = pltpu.make_async_remote_copy(
-            src_ref=fin_ref.at[slot_id],
-            dst_ref=fin_ref.at[slot_id],
-            send_sem=ga_send.at[other],
-            recv_sem=ga_recv.at[slot_id],
-            device_id={"region": other},
-            device_id_type=MESH,
-        )
-        if act == "start":
-            copy.start()
-        elif act == "recv":
-            copy.wait_recv()
-        else:
-            copy.wait_send()
-
-    for step in range(nr - 1):
-        spread_copy(step, "start")
+        for step in range(nr - 1):
+            spread_copy(chunk, step, "start")
+
     exchange(0, mic_out, mic_box, "sent")
     exchange(1, h1_out, h1_box, "sent")
     exchange(2, dz_out, dz_box, "sent")
@@ -491,8 +526,18 @@
         pl.when(me < CHUNKS)(lambda: for_each(nb - 1, lambda step: gather_copy(step, "sent")))
     else:
         for_each(nb - 1, lambda step: gather_copy(step, "sent"))
-    for step in range(nr - 1):
-        spread_copy(step, "recv")
+    for chunk in range(CHUNKS):
+        for step in range(nr - 1):
+            spread_copy(chunk, step, "recv")
+            spread_copy(chunk, step, "sent")
+
+
+def finish(
+    fin_ref, raw_ref, pred_ref, gw1_ref, gb1_ref, gw2_ref, gb2_ref, gwh_ref, gbh_ref
+):
+    nr, _, rows, _ = fin_ref.shape
+    channels = nr * rows
+    pred_ref[...] = raw_ref[...]
     for region in range(nr):
         where = slice(region * rows, (region + 1) * rows)
         for chunk in range(CHUNKS - 1):
@@ -507,14 +552,12 @@
     small = jnp.concatenate(
         [joined(fin_ref[region, CHUNKS - 1]) for region in range(nr)], axis=0
     )
-    gw1_ref[...] = small[:, :TAPS]
     turned = jnp.concatenate([small, jnp.zeros((128 - channels, 128), F32)], axis=0).T
+    gw1_ref[...] = turned[:TAPS, :channels]
     gb1_ref[...] = turned[27:28, :channels]
     gb2_ref[...] = turned[28:29, :channels]
     gbh_ref[...] = turned[29:30, :4]
     gwh_ref[...] = turned[32:36, :channels]
-    for step in range(nr - 1):
-        spread_copy(step, "sent")
 
 
 def solution(mesh):
@@ -531,21 +574,17 @@
             functools.partial(kernel, nb, nr, total_bricks),
             out_shape=(
                 jax.ShapeDtypeStruct((4, CELLS), BF16),
-                jax.ShapeDtypeStruct((channels, TAPS), F32),
-                jax.ShapeDtypeStruct((1, channels), F32),
-                jax.ShapeDtypeStruct((channels, TAPS * channels), F32),
-                jax.ShapeDtypeStruct((1, channels), F32),
-                jax.ShapeDtypeStruct((4, channels), F32),
-                jax.ShapeDtypeStruct((1, 4), F32),
+                jax.ShapeDtypeStruct((nr, CHUNKS, rows, CHUNK), BF16),
             ),
-            in_specs=[vmem, smem, smem] + [vmem] * 7,
-            out_specs=(vmem,) * 7,
+            in_specs=[vmem, smem, smem, vmem, vmem, pl.BlockSpec(memory_space=pl.ANY)] + [vmem] * 4,
+            out_specs=(vmem,) * 2,
             scratch_shapes=[
-                pltpu.VMEM((MAIN, CELLS), BF16),
-                pltpu.VMEM((MAIN, CELLS), BF16),
-                pltpu.VMEM((channels, 128), BF16),
+                pltpu.VMEM((WIDE, WIDE), BF16),
+                pltpu.VMEM((WIDE, WIDE), BF16),
+                pltpu.VMEM((128, channels), BF16),
                 pltpu.VMEM((channels, MAIN), BF16),
-                pltpu.VMEM((channels, MAIN), BF16),
+                pltpu.VMEM((3 * channels, WIDE), BF16),
+                pltpu.VMEM((3 * channels, WIDE), BF16),
                 pltpu.VMEM((128, CELLS), BF16),
                 pltpu.VMEM((CELLS, 128), BF16),
                 pltpu.VMEM((256, WIDE), BF16),
@@ -559,7 +598,8 @@
                 pltpu.VMEM((nr, rows, MAIN + CHUNK), BF16),
                 pltpu.VMEM((CHUNKS, rows, CHUNK), BF16),
                 pltpu.VMEM((nb, rows, CHUNK), BF16),
-                pltpu.VMEM((nr, CHUNKS, rows, CHUNK), BF16),
+                pltpu.VMEM((channels, TAPS * channels), BF16),
+                dma,
                 dma((3, 6)),
                 dma((3, 6)),
                 dma((2, nr)),
@@ -568,8 +608,8 @@
                 dma((nb,)),
                 dma((nb,)),
                 dma((CHUNKS,)),
-                dma((nr,)),
-                dma((nr,)),
+                dma((nr, CHUNKS)),
+                dma((nr, CHUNKS)),
             ],
             compiler_params=pltpu.CompilerParams(
                 collective_id=0, has_side_effects=True, vmem_limit_bytes=40 * 1024 * 1024
@@ -579,7 +619,7 @@
             mic.reshape(1, CELLS),
             tissue,
             neighbours.reshape(1, 26),
-            w1,
+            w1.T,
             b1.reshape(1, channels),
             w2,
             b2.reshape(1, channels),
@@ -587,10 +627,23 @@
             hb.reshape(1, 4),
             cot.reshape(4, CELLS),
         )
-        pred, gw1, gb1, gw2, gb2, gwh, gbh = outs
+        pred, gw1, gb1, gw2, gb2, gwh, gbh = pl.pallas_call(
+            finish,
+            out_shape=(
+                jax.ShapeDtypeStruct((4, CELLS), BF16),
+                jax.ShapeDtypeStruct((TAPS, channels), F32),
+                jax.ShapeDtypeStruct((1, channels), F32),
+                jax.ShapeDtypeStruct((channels, TAPS * channels), F32),
+                jax.ShapeDtypeStruct((1, channels), F32),
+                jax.ShapeDtypeStruct((4, channels), F32),
+                jax.ShapeDtypeStruct((1, 4), F32),
+            ),
+            in_specs=[vmem] * 2,
+            out_specs=(vmem,) * 7,
+        )(outs[1], outs[0])
         return (
             pred.reshape(1, 1, 4, CELLS),
-            gw1,
+            gw1.T,
             gb1.reshape(channels),
             gw2,
             gb2.reshape(channels),

time: 42.2 us -> 45.7 us (1.083)
  Pallas kernels: 34.7 us -> 38.5 us
    pallas_call x1, Pallas kernels: 34.7 us -> 36.7 us  [shards(): pl.pallas_call(functools.partial(kernel, nb, nr, total_bricks), out_shape...]
    pallas_call x0 -> x1, Pallas kernels: none -> 1.76 us  [shards(): pl.pallas_call(finish, out_shape=(jax.ShapeDtypeStruct((4, CELLS), BF16),...]
    unnamed x26 -> x22, local copies, waits for them, and re-layouts: 5.83 us -> 5.52 us
where the time goes in v2:
time: 45.7 us; the launch traced here: 45.4 us
  Pallas kernels  38.5 us (84%)
  local copies, waits for them, and re-layouts  5.52 us (12%)
  between operations  1.36 us (3%)
    pallas_call x1, Pallas kernels, shards(): pl.pallas_call(functools.partial(kernel, nb, nr, total_bricks), out_shape...  36.7 us
    unnamed x22, local copies, waits for them, and re-layouts  5.52 us
    pallas_call x1, Pallas kernels, shards(): pl.pallas_call(finish, out_shape=(jax.ShapeDtypeStruct((4, CELLS), BF16),...  1.76 us

profile of v2, /device:TPU:0, one launch (start us, length us, event | category | flops | bytes accessed | tf_op | source)
XLA Modules:
  0.0 45.4 jit_solution(6346511392477623673)
XLA Ops:
  0.6 0.0 copy-start.3
  1.3 0.0 copy-start.4
  1.3 0.0 copy-start.5
  1.3 0.0 copy-start.6
  1.3 0.0 copy-done.3
  1.3 0.6 %copy-done.4 = bf16[1,1,4,512]{3,2,1,0:T(4,128)(2,1)S(1)} copy-done((bf16[1,1,4,512]{3,2,1,0:T(4,128)(2,1)S(1)}, bf16[1,1,4,512]{3,2,1,0:T(4,128)(2,1)}, u32[]{:S(2)}) %copy-start.4) | copy-done | bytes 4120
  2.0 0.0 copy-done.5
  2.0 0.0 copy-done.6
  2.0 0.0 copy-start.2
  2.0 0.9 %copy-done.2 = bf16[64,1728]{1,0:T(8,128)(2,1)S(1)} copy-done((bf16[64,1728]{1,0:T(8,128)(2,1)S(1)}, bf16[64,1728]{1,0:T(8,128)(2,1)}, u32[]{:S(2)}) %copy-start.2) | copy-done | bytes 221208
  3.0 0.0 copy-start.7
  3.0 0.7 %copy-done.7 = s32[1,1,26]{2,1,0:T(1,128)S(1)} copy-done((s32[1,1,26]{2,1,0:T(1,128)S(1)}, s32[1,1,26]{2,1,0:T(1,128)}, u32[]{:S(2)}) %copy-start.7) | copy-done | bytes 128
  3.6 0.0 copy-start.8
  3.6 0.7 %copy-done.8 = f32[64]{0:T(128)S(1)} copy-done((f32[64]{0:T(128)S(1)}, f32[64]{0:T(128)}, u32[]{:S(2)}) %copy-start.8) | copy-done | bytes 280
  4.3 0.0 copy-start.9
  4.3 0.7 %copy-done.9 = f32[64]{0:T(128)S(1)} copy-done((f32[64]{0:T(128)S(1)}, f32[64]{0:T(128)}, u32[]{:S(2)}) %copy-start.9) | copy-done | bytes 280
  4.9 0.0 copy-start.10
  4.9 0.7 %copy-done.10 = f32[4]{0:T(128)S(1)} copy-done((f32[4]{0:T(128)S(1)}, f32[4]{0:T(128)}, u32[]{:S(2)}) %copy-start.10) | copy-done | bytes 40
  5.6 36.7 %shard_map.153 = (bf16[4,512]{1,0:T(4,128)(2,1)S(1)}, bf16[4,8,16,256]{3,2,1,0:T(8,128)(2,1)S(1)}) custom-call(bf16[1,512]{1,0:T(2,128)(2,1)S(1)} %bitcast.14, s32[1,1]{1,0:T(1,128)S(6)} %copy.17.tis_ref, s32[1,26]{1,0:T(1,128)S(1)} %bitcast.15, bf16[27,64]{1,0:T(8,128)(2,1)S(1)} %bitcast.12, f32[1,64]{1,0:T(1,128)S(1)} %bitcast.16, ...), custom_call_target="tpu_custom_call" | custom-call | flops 360000000 | bytes 2000000 | tf_op jit(solution)/shard_map/pallas_call | solution.py:573
  42.3 0.0 copy-start
  42.3 0.7 %copy-done = bf16[4,8,16,256]{3,2,1,0:T(8,128)(2,1)} copy-done((bf16[4,8,16,256]{3,2,1,0:T(8,128)(2,1)}, bf16[4,8,16,256]{3,2,1,0:T(8,128)(2,1)S(1)}, u32[]{:S(2)}) %copy-start) | copy-done | bytes 262168
  43.0 0.0 copy-start.1
  43.0 0.6 %copy-done.1 = bf16[4,512]{1,0:T(4,128)(2,1)} copy-done((bf16[4,512]{1,0:T(4,128)(2,1)}, bf16[4,512]{1,0:T(4,128)(2,1)S(1)}, u32[]{:S(2)}) %copy-start.1) | copy-done | bytes 4120
  43.6 1.8 %shard_map.154 = (bf16[4,512]{1,0:T(4,128)(2,1)}, f32[27,64]{1,0:T(8,128)}, f32[1,64]{1,0:T(1,128)}, f32[64,1728]{1,0:T(8,128)}, f32[1,64]{1,0:T(1,128)}, /*index=5*/f32[4,64]{1,0:T(4,128)}, f32[1,4]{1,0:T(1,128)}) custom-call(bf16[4,8,16,256]{3,2,1,0:T(8,128)(2,1)} %copy-done, bf16[4,512]{1,0:T(4,128)(2,1)} %copy-done.1), custom_call_target="tpu_custom_call" | custom-call | tf_op jit(solution)/shard_map/pallas_call | solution.py:630
Async XLA Ops:
  0.6 0.7 %copy-start.3 = (bf16[64,27]{0,1:T(8,128)(2,1)S(1)}, bf16[64,27]{0,1:T(8,128)(2,1)}, u32[]{:S(2)}) copy-start(bf16[64,27]{0,1:T(8,128)(2,1)} %param.13) | copy-start | bytes 10372
  1.3 0.7 %copy-start.4 = (bf16[1,1,4,512]{3,2,1,0:T(4,128)(2,1)S(1)}, bf16[1,1,4,512]{3,2,1,0:T(4,128)(2,1)}, u32[]{:S(2)}) copy-start(bf16[1,1,4,512]{3,2,1,0:T(4,128)(2,1)} %param.19) | copy-start | bytes 12292
  1.3 0.7 %copy-start.5 = (bf16[1,1,512]{2,1,0:T(2,128)(2,1)S(1)}, bf16[1,1,512]{2,1,0:T(2,128)(2,1)}, u32[]{:S(2)}) copy-start(bf16[1,1,512]{2,1,0:T(2,128)(2,1)} %param.10) | copy-start | bytes 3076
  1.3 0.7 %copy-start.6 = (bf16[4,64]{1,0:T(4,128)(2,1)S(1)}, bf16[4,64]{1,0:T(4,128)(2,1)}, u32[]{:S(2)}) copy-start(bf16[4,64]{1,0:T(4,128)(2,1)} %hw_ref.1) | copy-start | bytes 1540
  2.0 0.9 %copy-start.2 = (bf16[64,1728]{1,0:T(8,128)(2,1)S(1)}, bf16[64,1728]{1,0:T(8,128)(2,1)}, u32[]{:S(2)}) copy-start(bf16[64,1728]{1,0:T(8,128)(2,1)} %w2_ref.1) | copy-start | bytes 663556
  3.0 0.7 %copy-start.7 = (s32[1,1,26]{2,1,0:T(1,128)S(1)}, s32[1,1,26]{2,1,0:T(1,128)}, u32[]{:S(2)}) copy-start(s32[1,1,26]{2,1,0:T(1,128)} %param.12) | copy-start | bytes 316
  3.6 0.7 %copy-start.8 = (f32[64]{0:T(128)S(1)}, f32[64]{0:T(128)}, u32[]{:S(2)}) copy-start(f32[64]{0:T(128)} %param.14) | copy-start | bytes 772
  4.3 0.7 %copy-start.9 = (f32[64]{0:T(128)S(1)}, f32[64]{0:T(128)}, u32[]{:S(2)}) copy-start(f32[64]{0:T(128)} %param.16) | copy-start | bytes 772
  4.9 0.7 %copy-start.10 = (f32[4]{0:T(128)S(1)}, f32[4]{0:T(128)}, u32[]{:S(2)}) copy-start(f32[4]{0:T(128)} %param.18) | copy-start | bytes 52
  42.3 0.7 %copy-start = (bf16[4,8,16,256]{3,2,1,0:T(8,128)(2,1)}, bf16[4,8,16,256]{3,2,1,0:T(8,128)(2,1)S(1)}, u32[]{:S(2)}) copy-start(bf16[4,8,16,256]{3,2,1,0:T(8,128)(2,1)S(1)} %get-tuple-element.16.fin_ref) | copy-start | bytes 786436
  43.0 0.6 %copy-start.1 = (bf16[4,512]{1,0:T(4,128)(2,1)}, bf16[4,512]{1,0:T(4,128)(2,1)S(1)}, u32[]{:S(2)}) copy-start(bf16[4,512]{1,0:T(4,128)(2,1)S(1)} %get-tuple-element.17.raw_ref) | copy-start | bytes 12292

commit v3 on v2

--- a/solution.py
+++ b/solution.py
@@ -113,9 +113,9 @@
 
 
 def windows(padded, halo, emit):
-    lane = iota(padded.shape, 1)
-    z = lane % 8
-    y = (lane // 8) % 8
+    row = iota((1, WIDE), 1)
+    z = jnp.broadcast_to(row & 7, padded.shape)
+    y = jnp.broadcast_to(row & 56, padded.shape)
     for c in (-1, 0, 1):
         if c == 0:
             along = padded
@@ -125,23 +125,23 @@
             along = jnp.where(z == 0, halo, pltpu.roll(padded, 1, 1))
         emit(3 + c + 1, along)
         emit(c + 1, jnp.where(y == 0, 0.0, pltpu.roll(along, 8, 1)))
-        emit(6 + c + 1, jnp.where(y == 7, 0.0, pltpu.roll(along, WIDE - 8, 1)))
+        emit(6 + c + 1, jnp.where(y == 56, 0.0, pltpu.roll(along, WIDE - 8, 1)))
 
 
 def kernel(
     nb,
     nr,
     total_bricks,
-    mic_ref,
+    mic_hbm,
     tis_ref,
     nei_ref,
-    w1_ref,
-    b1_ref,
-    w2_ref,
-    b2_ref,
-    hw_ref,
-    hb_ref,
-    cot_ref,
+    w1_hbm,
+    b1_hbm,
+    w2_hbm,
+    b2_hbm,
+    hw_hbm,
+    hb_hbm,
+    cot_hbm,
     pred_ref,
     fin_ref,
     s1_ref,
@@ -163,8 +163,15 @@
     ra_ref,
     rb_src,
     rb_ref,
-    w2_box,
-    w2_sem,
+    mic_ref,
+    w1_ref,
+    b1_ref,
+    w2_ref,
+    b2_ref,
+    hw_ref,
+    hb_ref,
+    cot_ref,
+    in_sem,
     ex_send,
     ex_recv,
     a_send,
@@ -181,8 +188,13 @@
     channels = w2_ref.shape[0]
     rows = channels // nr
 
-    fetch = pltpu.make_async_copy(w2_ref, w2_box, w2_sem)
-    fetch.start()
+    sources = (mic_hbm, w1_hbm, b1_hbm, w2_hbm, b2_hbm, hw_hbm, hb_hbm, cot_hbm)
+    places = (mic_ref, w1_ref, b1_ref, w2_ref, b2_ref, hw_ref, hb_ref, cot_ref)
+    fetches = [
+        pltpu.make_async_copy(source, place, in_sem.at[k])
+        for k, (source, place) in enumerate(zip(sources, places))
+    ]
+    fetches[0].start()
     for box in (mic_box, h1_box, dz_box):
         box[...] = jnp.zeros_like(box)
 
@@ -199,11 +211,15 @@
             barrier, inc=1, device_id={"region": (mr + 1 + step) % nr}, device_id_type=MESH
         )
 
+    for fetch in fetches[1:]:
+        fetch.start()
+
     spot, slot = iota((CELLS, 128), 0), iota((CELLS, 128), 1)
     pick_ref[...] = jnp.where(
-        spot == (slot % PLANE) * 8 + 7 * (slot // PLANE), 1.0, 0.0
+        spot == (slot & 63) * 8 + 7 * (slot >> 6), 1.0, 0.0
     ).astype(BF16)
     pick = pick_ref[...]
+    fetches[0].wait()
     mic = jnp.broadcast_to(mic_ref[...].astype(F32), (MIC_ROWS, CELLS))
     pack(mic, pick, mic_out)
 
@@ -243,15 +259,16 @@
 
     spread_row, spread_lane = iota((256, WIDE), 0), iota((256, WIDE), 1)
     spread_ref[...] = jnp.where(
-        spread_lane == (spread_row % 128) * 8 + 7 * (1 - spread_row // 128), 1.0, 0.0
+        spread_lane == (spread_row & 127) * 8 + 7 - 7 * (spread_row >> 7), 1.0, 0.0
     ).astype(BF16)
+    for fetch in fetches[1:]:
+        fetch.wait()
     w1p_ref[...] = jnp.zeros_like(w1p_ref)
     w1p_ref[:TAPS, :] = w1_ref[...]
     s1_ref[9 * channels :, :] = jnp.zeros((channels, WIDE), BF16)
     s2_ref[9 * channels :, :] = jnp.zeros((channels, WIDE), BF16)
-    fetch.wait()
     w2p_ref[:, MAIN - 128 :] = jnp.zeros((channels, 128), BF16)
-    w2p_ref[:, : TAPS * channels] = w2_box[...]
+    w2p_ref[:, : TAPS * channels] = w2_ref[...]
     taps_lane = iota((channels, WIDE), 1) < 9 * channels
     for a in range(3):
         view = w2p_ref[:, 512 * a + 64 * a - 64 * (a % 2) : 512 * a + 64 * a - 64 * (a % 2) + WIDE]
@@ -567,6 +584,7 @@
         channels = w1.shape[0]
         rows = channels // nr
         vmem = pl.BlockSpec(memory_space=pltpu.VMEM)
+        hbm = pl.BlockSpec(memory_space=pl.ANY)
         smem = pl.BlockSpec(memory_space=pltpu.SMEM)
         dma = pltpu.SemaphoreType.DMA
         total_bricks = nb * nr * mic.shape[1]
@@ -576,7 +594,7 @@
                 jax.ShapeDtypeStruct((4, CELLS), BF16),
                 jax.ShapeDtypeStruct((nr, CHUNKS, rows, CHUNK), BF16),
             ),
-            in_specs=[vmem, smem, smem, vmem, vmem, pl.BlockSpec(memory_space=pl.ANY)] + [vmem] * 4,
+            in_specs=[hbm, smem, smem] + [hbm] * 7,
             out_specs=(vmem,) * 2,
             scratch_shapes=[
                 pltpu.VMEM((WIDE, WIDE), BF16),
@@ -598,8 +616,15 @@
                 pltpu.VMEM((nr, rows, MAIN + CHUNK), BF16),
                 pltpu.VMEM((CHUNKS, rows, CHUNK), BF16),
                 pltpu.VMEM((nb, rows, CHUNK), BF16),
+                pltpu.VMEM((1, CELLS), BF16),
+                pltpu.VMEM((TAPS, channels), BF16),
+                pltpu.VMEM((1, channels), F32),
                 pltpu.VMEM((channels, TAPS * channels), BF16),
-                dma,
+                pltpu.VMEM((1, channels), F32),
+                pltpu.VMEM((4, channels), BF16),
+                pltpu.VMEM((1, 4), F32),
+                pltpu.VMEM((4, CELLS), BF16),
+                dma((8,)),
                 dma((3, 6)),
                 dma((3, 6)),
                 dma((2, nr)),
@@ -612,7 +637,7 @@
                 dma((nr, CHUNKS)),
             ],
             compiler_params=pltpu.CompilerParams(
-                collective_id=0, has_side_effects=True, vmem_limit_bytes=40 * 1024 * 1024
+                collective_id=0, has_side_effects=True, vmem_limit_bytes=60 * 1024 * 1024
             ),
             cost_estimate=pl.CostEstimate(flops=360_000_000, bytes_accessed=2_000_000, transcendentals=65536),
         )(
@@ -640,6 +665,7 @@
             ),
             in_specs=[vmem] * 2,
             out_specs=(vmem,) * 7,
+            compiler_params=pltpu.CompilerParams(vmem_limit_bytes=60 * 1024 * 1024),
         )(outs[1], outs[0])
         return (
             pred.reshape(1, 1, 4, CELLS),

time: 45.7 us -> 40.6 us (0.89)
  local copies, waits for them, and re-layouts: 5.52 us -> 0 us
  Pallas kernels: 38.5 us -> 39.1 us
    unnamed x22 -> x0, local copies, waits for them, and re-layouts: 5.52 us -> none
    pallas_call x1, Pallas kernels: 36.7 us -> 37.3 us  [shards(): pl.pallas_call(functools.partial(kernel, nb, nr, total_bricks), out_shape...]
where the time goes in v3:
time: 40.6 us; the launch traced here: 40.4 us
  Pallas kernels  39.1 us (96%)
  between operations  1.29 us (3%)
    pallas_call x1, Pallas kernels, shards(): pl.pallas_call(functools.partial(kernel, nb, nr, total_bricks), out_shape...  37.3 us
    pallas_call x1, Pallas kernels, shards(): pl.pallas_call(finish, out_shape=(jax.ShapeDtypeStruct((4, CELLS), BF16),...  1.76 us

profile of v3, /device:TPU:0, one launch (start us, length us, event | category | flops | bytes accessed | tf_op | source)
XLA Modules:
  0.0 40.4 jit_solution(1904321489485669666)
XLA Ops:
  1.3 37.3 %shard_map.153 = (bf16[4,512]{1,0:T(4,128)(2,1)}, bf16[4,8,16,256]{3,2,1,0:T(8,128)(2,1)}) custom-call(bf16[1,512]{1,0:T(2,128)(2,1)} %bitcast.16, s32[1,1]{1,0:T(1,128)S(6)} %copy.17.tis_ref, s32[1,26]{1,0:T(1,128)} %bitcast.17, bf16[27,64]{1,0:T(8,128)(2,1)} %bitcast.13, f32[1,64]{1,0:T(1,128)} %bitcast.18, bf16[64,1728]{1,0:T(8,128)(2,1)} %w2_hbm.1, ...), custom_call_target="tpu_custom_call" | custom-call | flops 360000000 | bytes 2000000 | tf_op jit(solution)/shard_map/pallas_call | solution.py:591
  38.6 1.8 %shard_map.154 = (bf16[4,512]{1,0:T(4,128)(2,1)}, f32[27,64]{1,0:T(8,128)}, f32[1,64]{1,0:T(1,128)}, f32[64,1728]{1,0:T(8,128)}, f32[1,64]{1,0:T(1,128)}, /*index=5*/f32[4,64]{1,0:T(4,128)}, f32[1,4]{1,0:T(1,128)}) custom-call(bf16[4,8,16,256]{3,2,1,0:T(8,128)(2,1)} %get-tuple-element.16.fin_ref, bf16[4,512]{1,0:T(4,128)(2,1)} %get-tuple-element.17.raw_ref), custom_call_target="tpu_custom_call" | custom-call | tf_op jit(solution)/shard_map/pallas_call | solution.py:655

commit v4 on v3

--- a/solution.py
+++ b/solution.py
@@ -142,8 +142,11 @@
     hw_hbm,
     hb_hbm,
     cot_hbm,
+    pred_out,
+    fin_out,
     pred_ref,
     fin_ref,
+    few_ref,
     s1_ref,
     s2_ref,
     w1p_ref,
@@ -172,6 +175,9 @@
     hb_ref,
     cot_ref,
     in_sem,
+    out_sem,
+    few_send,
+    few_recv,
     ex_send,
     ex_recv,
     a_send,
@@ -405,6 +411,8 @@
     h2 = (value2 * active).astype(BF16)
     linear = dot(hw_ref[...], h2) + bias3
     pred_ref[...] = (linear * active).astype(BF16)
+    pred_copy = pltpu.make_async_copy(pred_ref, pred_out, out_sem.at[CHUNKS])
+    pred_copy.start()
     tap_rows = a_ref[...]
     dpred_tall = jnp.concatenate(
         [dpred_wide, jnp.zeros((channels - 8, CELLS), F32)], axis=0
@@ -457,8 +465,8 @@
     def gather_copy(step, act):
         other = (me + 1 + step) % nb
         copy = pltpu.make_async_remote_copy(
-            src_ref=fin_ref.at[mr, me % CHUNKS],
-            dst_ref=fin_ref.at[mr, me % CHUNKS],
+            src_ref=fin_ref.at[me % CHUNKS],
+            dst_ref=fin_ref.at[me % CHUNKS],
             send_sem=gb_send.at[other],
             recv_sem=gb_recv.at[me % CHUNKS],
             device_id={"brick": other},
@@ -469,7 +477,7 @@
         else:
             copy.wait_send()
 
-    def own(final):
+    def own():
         def arrived(step):
             other = (me + 1 + step) % nb
             pltpu.make_async_remote_copy(
@@ -490,15 +498,15 @@
             kept = lax.fori_loop(
                 0, nb - 1, lambda step, s: s + rb_ref[(me + 1 + step) % nb].astype(F32), kept
             )
-        fin_ref[mr, me % CHUNKS] = halves(joined(kept)) if final else kept.astype(BF16)
+        fin_ref[me % CHUNKS] = kept.astype(BF16)
         for_each(nb - 1, lambda step: gather_copy(step, "start"))
 
     def spread_copy(chunk, step, act):
         other = (mr + 1 + step) % nr
         slot_id = other if act == "recv" else mr
         copy = pltpu.make_async_remote_copy(
-            src_ref=fin_ref.at[slot_id, chunk],
-            dst_ref=fin_ref.at[slot_id, chunk],
+            src_ref=fin_ref.at[chunk],
+            dst_ref=fin_out.at[slot_id, chunk],
             send_sem=ga_send.at[other, chunk],
             recv_sem=ga_recv.at[slot_id, chunk],
             device_id={"region": other},
@@ -511,25 +519,62 @@
         else:
             copy.wait_send()
 
-    pl.when(me < CHUNKS - 1)(lambda: own(False))
-    rb_src[CHUNKS - 1] = halves(joined(region_sum(1)))
-    brick_copy(CHUNKS - 1, "start")
-    pl.when(me == CHUNKS - 1)(lambda: own(True))
-
-    for chunk in range(CHUNKS):
+    pl.when(me < CHUNKS - 1)(own)
+
+    def few_copy(step, act):
+        other = (me + 1 + step) % nb
+        slot_id = other if act == "recv" else me
+        copy = pltpu.make_async_remote_copy(
+            src_ref=rb_src.at[CHUNKS - 1],
+            dst_ref=few_ref.at[slot_id],
+            send_sem=few_send.at[other],
+            recv_sem=few_recv.at[slot_id],
+            device_id={"brick": other},
+            device_id_type=MESH,
+        )
+        if act == "start":
+            copy.start()
+        elif act == "recv":
+            copy.wait_recv()
+        else:
+            copy.wait_send()
+
+    few = halves(joined(region_sum(1)))
+    rb_src[CHUNKS - 1] = few
+    for_each(nb - 1, lambda step: few_copy(step, "start"))
+    few_ref[me] = few
+
+    def keep(chunk):
+        return pltpu.make_async_copy(fin_ref.at[chunk], fin_out.at[mr, chunk], out_sem.at[chunk])
+
+    def pass_on(chunk):
+        for step in range(nr - 1):
+            spread_copy(chunk, step, "start")
+        keep(chunk).start()
+
+    for chunk in range(CHUNKS - 1):
         @pl.when(me != chunk)
         def _():
             pltpu.make_async_remote_copy(
-                src_ref=fin_ref.at[mr, chunk],
-                dst_ref=fin_ref.at[mr, chunk],
+                src_ref=fin_ref.at[chunk],
+                dst_ref=fin_ref.at[chunk],
                 send_sem=gb_send.at[chunk],
                 recv_sem=gb_recv.at[chunk],
                 device_id={"brick": chunk},
                 device_id_type=MESH,
             ).wait_recv()
 
-        for step in range(nr - 1):
-            spread_copy(chunk, step, "start")
+        pass_on(chunk)
+
+    for_each(nb - 1, lambda step: few_copy(step, "recv"))
+    if nb <= CHUNKS:
+        few = joined(few_ref[0])
+        for brick in range(1, nb):
+            few = few + joined(few_ref[brick])
+    else:
+        few = lax.fori_loop(1, nb, lambda brick, s: s + joined(few_ref[brick]), joined(few_ref[0]))
+    fin_ref[CHUNKS - 1] = halves(few)
+    pass_on(CHUNKS - 1)
 
     exchange(0, mic_out, mic_box, "sent")
     exchange(1, h1_out, h1_box, "sent")
@@ -537,12 +582,13 @@
     for part in range(2):
         for step in range(nr - 1):
             region_copy(part, step, "sent")
+    for chunk in range(CHUNKS - 1):
+        brick_copy(chunk, "sent")
+    pl.when(me < CHUNKS - 1)(lambda: for_each(nb - 1, lambda step: gather_copy(step, "sent")))
+    for_each(nb - 1, lambda step: few_copy(step, "sent"))
+    pred_copy.wait()
     for chunk in range(CHUNKS):
-        brick_copy(chunk, "sent")
-    if nb > CHUNKS:
-        pl.when(me < CHUNKS)(lambda: for_each(nb - 1, lambda step: gather_copy(step, "sent")))
-    else:
-        for_each(nb - 1, lambda step: gather_copy(step, "sent"))
+        keep(chunk).wait()
     for chunk in range(CHUNKS):
         for step in range(nr - 1):
             spread_copy(chunk, step, "recv")
@@ -595,8 +641,11 @@
                 jax.ShapeDtypeStruct((nr, CHUNKS, rows, CHUNK), BF16),
             ),
             in_specs=[hbm, smem, smem] + [hbm] * 7,
-            out_specs=(vmem,) * 2,
+            out_specs=(hbm,) * 2,
             scratch_shapes=[
+                pltpu.VMEM((4, CELLS), BF16),
+                pltpu.VMEM((CHUNKS, rows, CHUNK), BF16),
+                pltpu.VMEM((nb, rows, CHUNK), BF16),
                 pltpu.VMEM((WIDE, WIDE), BF16),
                 pltpu.VMEM((WIDE, WIDE), BF16),
                 pltpu.VMEM((128, channels), BF16),
@@ -625,6 +674,9 @@
                 pltpu.VMEM((1, 4), F32),
                 pltpu.VMEM((4, CELLS), BF16),
                 dma((8,)),
+                dma((CHUNKS + 1,)),
+                dma((nb,)),
+                dma((nb,)),
                 dma((3, 6)),
                 dma((3, 6)),
                 dma((2, nr)),

time: 40.6 us -> 36 us (0.89)
  Pallas kernels: 39.1 us -> 34.6 us
    pallas_call x1, Pallas kernels: 37.3 us -> 32.8 us  [shards(): pl.pallas_call(functools.partial(kernel, nb, nr, total_bricks), out_shape...]
where the time goes in v4:
time: 36 us; the launch traced here: 35.9 us
  Pallas kernels  34.6 us (96%)
  between operations  1.29 us (4%)
    pallas_call x1, Pallas kernels, shards(): pl.pallas_call(functools.partial(kernel, nb, nr, total_bricks), out_shape...  32.8 us
    pallas_call x1, Pallas kernels, shards(): pl.pallas_call(finish, out_shape=(jax.ShapeDtypeStruct((4, CELLS), BF16),...  1.76 us

profile of v4, /device:TPU:0, one launch (start us, length us, event | category | flops | bytes accessed | tf_op | source)
XLA Modules:
  0.0 35.9 jit_solution(14703641816266154460)
XLA Ops:
  1.3 32.8 %shard_map.153 = (bf16[4,512]{1,0:T(4,128)(2,1)}, bf16[4,8,16,256]{3,2,1,0:T(8,128)(2,1)}) custom-call(bf16[1,512]{1,0:T(2,128)(2,1)} %bitcast.16, s32[1,1]{1,0:T(1,128)S(6)} %copy.17.tis_ref, s32[1,26]{1,0:T(1,128)} %bitcast.17, bf16[27,64]{1,0:T(8,128)(2,1)} %bitcast.13, f32[1,64]{1,0:T(1,128)} %bitcast.18, bf16[64,1728]{1,0:T(8,128)(2,1)} %w2_hbm.1, ...), custom_call_target="tpu_custom_call" | custom-call | flops 360000000 | bytes 2000000 | tf_op jit(solution)/shard_map/pallas_call | solution.py:637
  34.1 1.8 %shard_map.154 = (bf16[4,512]{1,0:T(4,128)(2,1)}, f32[27,64]{1,0:T(8,128)}, f32[1,64]{1,0:T(1,128)}, f32[64,1728]{1,0:T(8,128)}, f32[1,64]{1,0:T(1,128)}, /*index=5*/f32[4,64]{1,0:T(4,128)}, f32[1,4]{1,0:T(1,128)}) custom-call(bf16[4,8,16,256]{3,2,1,0:T(8,128)(2,1)} %get-tuple-element.16.fin_ref, bf16[4,512]{1,0:T(4,128)(2,1)} %get-tuple-element.17.raw_ref), custom_call_target="tpu_custom_call" | custom-call | tf_op jit(solution)/shard_map/pallas_call | solution.py:707

commit v5 on v4

--- a/solution.py
+++ b/solution.py
@@ -452,15 +452,15 @@
     exchange(2, dz_out, dz_box, "recv")
     padded, halo = widen(dz2.astype(F32), dz_box, flags, spread)
     windows(padded, halo, store_windows(s2_ref))
-    total = region_sum(0)
-    for chunk in range(CHUNKS - 1):
-        rb_src[chunk] = total[:, CHUNK * chunk : CHUNK * (chunk + 1)].astype(BF16)
-        brick_copy(chunk, "start")
     dz1 = (convolve(back_ref, s2_ref) * slope1).astype(BF16)
     small = small + jnp.where(lane < 28, dot_nt(dz1, tap_rows), 0.0)
     grad_ref[:, MAIN:] = halves(small)
     for step in range(nr - 1):
         region_copy(1, step, "start")
+    total = region_sum(0)
+    for chunk in range(CHUNKS - 1):
+        rb_src[chunk] = total[:, CHUNK * chunk : CHUNK * (chunk + 1)].astype(BF16)
+        brick_copy(chunk, "start")
 
     def gather_copy(step, act):
         other = (me + 1 + step) % nb

time: 36 us -> 36.5 us (1.014)
  Pallas kernels: 34.6 us -> 35.1 us
    pallas_call x1, Pallas kernels: 32.8 us -> 33.3 us  [shards(): pl.pallas_call(functools.partial(kernel, nb, nr, total_bricks), out_shape...]
where the time goes in v5:
time: 36.5 us; the launch traced here: 36.4 us
  Pallas kernels  35.1 us (96%)
  between operations  1.29 us (4%)
    pallas_call x1, Pallas kernels, shards(): pl.pallas_call(functools.partial(kernel, nb, nr, total_bricks), out_shape...  33.3 us
    pallas_call x1, Pallas kernels, shards(): pl.pallas_call(finish, out_shape=(jax.ShapeDtypeStruct((4, CELLS), BF16),...  1.76 us

profile of v5, /device:TPU:0, one launch (start us, length us, event | category | flops | bytes accessed | tf_op | source)
XLA Modules:
  0.0 36.4 jit_solution(17311368567628999230)
XLA Ops:
  1.3 33.3 %shard_map.153 = (bf16[4,512]{1,0:T(4,128)(2,1)}, bf16[4,8,16,256]{3,2,1,0:T(8,128)(2,1)}) custom-call(bf16[1,512]{1,0:T(2,128)(2,1)} %bitcast.16, s32[1,1]{1,0:T(1,128)S(6)} %copy.17.tis_ref, s32[1,26]{1,0:T(1,128)} %bitcast.17, bf16[27,64]{1,0:T(8,128)(2,1)} %bitcast.13, f32[1,64]{1,0:T(1,128)} %bitcast.18, bf16[64,1728]{1,0:T(8,128)(2,1)} %w2_hbm.1, ...), custom_call_target="tpu_custom_call" | custom-call | flops 360000000 | bytes 2000000 | tf_op jit(solution)/shard_map/pallas_call | solution.py:637
  34.6 1.8 %shard_map.154 = (bf16[4,512]{1,0:T(4,128)(2,1)}, f32[27,64]{1,0:T(8,128)}, f32[1,64]{1,0:T(1,128)}, f32[64,1728]{1,0:T(8,128)}, f32[1,64]{1,0:T(1,128)}, /*index=5*/f32[4,64]{1,0:T(4,128)}, f32[1,4]{1,0:T(1,128)}) custom-call(bf16[4,8,16,256]{3,2,1,0:T(8,128)(2,1)} %get-tuple-element.16.fin_ref, bf16[4,512]{1,0:T(4,128)(2,1)} %get-tuple-element.17.raw_ref), custom_call_target="tpu_custom_call" | custom-call | tf_op jit(solution)/shard_map/pallas_call | solution.py:707
